TPU v7x, 32 devices: a whole 2x2x4 slice. The times are simulated.
32 devices in a mesh: dp: 8 (over z, y), seq: 4 (over x, core).
Axes of the slice: x: 2, y: 2, z: 4, core: 2. Of those that a mesh axis runs over, the one named last changes fastest.
Arguments:
- tokens: bfloat16 [16, 1024, 1536], P('dp', 'seq'), may hold values from -8 to 8
- segment_ids: int32 [16, 1024], P('dp'), may hold values from 0 to 32, as said below
- w_in: bfloat16 [1536, 6448], P('dp'), may hold values from -0.15625 to 0.15625
- w_out: bfloat16 [3072, 1536], P('dp'), may hold values from -0.109375 to 0.109375
- conv_weight: bfloat16 [3328, 4], P('dp'), may hold values from -3 to 3
- conv_bias: bfloat16 [3328], P('dp'), may hold values from -1.75 to 1.75
- norm_gain: bfloat16 [1536], P('dp'), may hold values from 0.5 to 1.5
- gated_gain: bfloat16 [3072], P('dp'), may hold values from 0.5 to 1.5
- dt_bias: float32 [48], replicated, may hold values from -7 to -2.5
- a_log: float32 [48], replicated, may hold values from 0 to 2.77
- skip_weight: float32 [48], replicated, may hold values from 0.5 to 1.5
- cotangent: bfloat16 [16, 1024, 1536], P('dp', 'seq'), may hold values from -6 to 6
Outputs:
- out: bfloat16 [16, 1024, 1536], P('dp', 'seq')
- tokens_grad: float32 [16, 1024, 1536], P('dp', 'seq')
- w_in_grad: float32 [1536, 6448], P('dp')
- w_out_grad: float32 [3072, 1536], P('dp')
- conv_weight_grad: float32 [3328, 4], P('dp')
- conv_bias_grad: float32 [3328], P('dp')
- norm_gain_grad: float32 [1536], P('dp')
- gated_gain_grad: float32 [3072], P('dp')
- dt_bias_grad: float32 [48], replicated
- a_log_grad: float32 [48], replicated
- skip_weight_grad: float32 [48], replicated
Inputs may be any that keep to these rules, and one draw needn't show every extreme that they name: `segment_ids`: each row starts at 0 and rises by 0 or 1 from one token to the next; in each aligned group of 2 rows one row, which one varies, is a single document.
All inputs are finite; a program needn't handle non-finite values.
Results may differ from a plain program's by a relative error of at most 0.015.
Values may be sent and summed in bfloat16 or wider, within the bound.
A program may use at most 256 MiB of HBM per device.

v0:
```python
import functools

import jax
import jax.numpy as jnp
from jax import lax
from jax.experimental import pallas as pl
from jax.experimental.pallas import tpu as pltpu
from jax.sharding import PartitionSpec as P

Q = 128
EXACT = lax.Precision.HIGHEST
EPSILON = 1e-05
LOG2E = 1.4426950408889634
RESET = 160.0
F32 = jnp.float32
BF16 = jnp.bfloat16
LUMPS = 6
WOFF = 1
MESH = pl.DeviceIdType.MESH


def sigmoid(x):
    return 0.5 * jnp.tanh(0.5 * x) + 0.5


def softplus(x):
    return jnp.maximum(x, 0.0) + jnp.log1p(jnp.exp(-jnp.abs(x)))


def nt(a, b):
    return lax.dot_general(a, b, (((1,), (1,)), ((), ())), preferred_element_type=F32)


def mm(a, b):
    return jnp.dot(a, b, preferred_element_type=F32)


def decays(pj, tall, hp, width):
    arg = pj[0, :, width + 256 : width + 384].astype(F32) + hp[0:1, :]
    dt = softplus(arg)
    rows = lax.broadcasted_iota(jnp.int32, (Q, Q), 0)
    lanes = lax.broadcasted_iota(jnp.int32, (Q, Q), 1)
    lower = (rows >= lanes).astype(F32)
    level = jnp.dot(lower, dt * hp[1:2, :], precision=EXACT, preferred_element_type=F32)
    level = level + tall[:, 3:4]
    return arg, dt, level, rows, lanes


def fwd_kernel(pairs, pj, marks, sg, hp, ch, pre, ys, st, red, state, tail):
    width = pairs * 256
    inner = pairs * 128
    chunk = pl.program_id(1)

    @pl.when(chunk == 0)
    def _():
        state[...] = jnp.zeros_like(state)
        tail[...] = jnp.zeros_like(tail)

    tall = jnp.concatenate([marks[0], jnp.zeros((Q - 8, Q), F32)], axis=0).T
    _, dt, level, rows, lanes = decays(pj, tall, hp, width)
    level_t = level.T
    low = lanes < 64
    masks = [tall[:, d : d + 1] for d in range(3)]

    def conv(raw, at):
        ext = jnp.concatenate([tail[:, at : at + 128], raw], axis=0)
        total = raw * ch[3:4, at : at + 128] + ch[4:5, at : at + 128]
        for d in (1, 2, 3):
            moved = pltpu.roll(ext, d, 0)[8:]
            total = total + moved * masks[d - 1] * ch[3 - d : 4 - d, at : at + 128]
        tail[:, at : at + 128] = raw[Q - 8 :]
        pre[0, :, at : at + 128] = total
        return total * sigmoid(total)

    b_rows = conv(pj[0, :, width : width + 128].astype(F32), inner)
    c_rows = conv(pj[0, :, width + 128 : width + 256].astype(F32), inner + 128)
    b_t = b_rows.T.astype(BF16)
    b_low = b_rows.astype(BF16)
    c_low = c_rows.astype(BF16)
    scores = jnp.where(rows >= lanes, nt(c_low, b_low), 0.0)
    old = state[...].astype(BF16)
    st[0, 0] = old
    carried_all = mm(c_low, old)
    squares = jnp.zeros((Q, 128), F32)
    cross = jnp.zeros((Q, 128), F32)
    for p in range(pairs):
        at = p * 128
        one = pj[0, :, p * 256 : p * 256 + 128].astype(F32)
        two = pj[0, :, p * 256 + 128 : p * 256 + 256].astype(F32)
        z = jnp.where(low, one, pltpu.roll(two, 64, 1))
        v = jnp.where(low, pltpu.roll(one, 64, 1), two)
        xc = conv(v, at)
        l0 = jnp.broadcast_to(level[:, 2 * p : 2 * p + 1], (Q, Q))
        l1 = jnp.broadcast_to(level[:, 2 * p + 1 : 2 * p + 2], (Q, Q))
        le = jnp.where(low, l0, l1)
        dte = jnp.where(low, dt[:, 2 * p : 2 * p + 1], dt[:, 2 * p + 1 : 2 * p + 2])
        u = xc * dte
        w0 = jnp.exp2(jnp.minimum(l0 - level_t[2 * p : 2 * p + 1, :], 0.0)) * scores
        w1 = jnp.exp2(jnp.minimum(l1 - level_t[2 * p + 1 : 2 * p + 2, :], 0.0)) * scores
        wide = jnp.concatenate([w0.astype(BF16), w1.astype(BF16)], axis=1)
        blocks = jnp.concatenate(
            [jnp.where(low, u, 0.0).astype(BF16), jnp.where(low, 0.0, u).astype(BF16)], axis=0
        )
        part = mm(wide, blocks) + carried_all[:, at : at + 128] * jnp.exp2(le)
        ys[0, :, at : at + 128] = part
        gated = (part + ch[5:6, at : at + 128] * xc) * (z * sigmoid(z))
        scaled = gated * ch[6:7, at : at + 128]
        squares = squares + gated * gated
        cross = cross + sg[0, :, at : at + 128].astype(F32) * scaled
        last = le[Q - 1 : Q, :]
        ul = (u * jnp.exp2(last - le)).astype(BF16)
        state[:, at : at + 128] = state[:, at : at + 128] * jnp.exp2(last) + mm(b_t, ul)
    both = jnp.where(
        lanes == 0, jnp.sum(squares, axis=1, keepdims=True), jnp.sum(cross, axis=1, keepdims=True)
    )
    red[0] = both.T[0:8]


def mix_forward(pj, marks, sg, hp, ch):
    seqs, length, total = pj.shape
    width = total - 384
    inner = width // 2
    pairs = inner // 128
    chunks = length // Q

    def row(n):
        return pl.BlockSpec((1, Q, n), lambda s, c: (s, c, 0))

    def whole(a):
        return pl.BlockSpec(a.shape, lambda s, c: (0,) * a.ndim)

    return pl.pallas_call(
        functools.partial(fwd_kernel, pairs),
        grid=(seqs, chunks),
        in_specs=[
            row(total),
            pl.BlockSpec((1, 8, Q), lambda s, c: (s, 0, c)),
            row(inner),
            whole(hp),
            whole(ch),
        ],
        out_specs=[
            row(inner + 256),
            row(inner),
            pl.BlockSpec((1, 1, 128, inner), lambda s, c: (s, c, 0, 0)),
            pl.BlockSpec((1, 8, Q), lambda s, c: (s, 0, c)),
        ],
        out_shape=[
            jax.ShapeDtypeStruct((seqs, length, inner + 256), F32),
            jax.ShapeDtypeStruct((seqs, length, inner), F32),
            jax.ShapeDtypeStruct((seqs, chunks, 128, inner), BF16),
            jax.ShapeDtypeStruct((seqs, 8, length), F32),
        ],
        scratch_shapes=[pltpu.VMEM((128, inner), F32), pltpu.VMEM((8, inner + 256), F32)],
        compiler_params=pltpu.CompilerParams(vmem_limit_bytes=60 * 2**20),
        name="mix_forward",
    )(pj, marks, sg, hp, ch)


def bwd_kernel(
    pairs, pj, marks, rk, sg, pre, ys, st, hp, ch, sel, pg, chacc, hacc, sct, scl,
    dstate, halo, edy_all, ul_all,
):
    width = pairs * 256
    inner = pairs * 128
    first = (pl.program_id(0) == 0) & (pl.program_id(1) == 0)

    @pl.when(pl.program_id(1) == 0)
    def _():
        dstate[...] = jnp.zeros_like(dstate)
        halo[...] = jnp.zeros_like(halo)

    @pl.when(first)
    def _():
        chacc[...] = jnp.zeros_like(chacc)
        hacc[...] = jnp.zeros_like(hacc)

    tall = jnp.concatenate([marks[0], rk[0], jnp.zeros((Q - 16, Q), F32)], axis=0).T
    arg, dt, level, rows, lanes = decays(pj, tall, hp, width)
    level_t = level.T
    low = lanes < 64
    masks = [tall[:, 3 + d : 4 + d] for d in (1, 2, 3)]
    rho = jnp.broadcast_to(tall[:, 8:9], (Q, 128))
    k2 = jnp.broadcast_to(tall[:, 9:10], (Q, 128))

    def fold(x):
        return jnp.sum(x.reshape(Q // 8, 8, 128), axis=0)

    def conv_back(grad, raw, at):
        ext = jnp.concatenate([grad, halo[:, at : at + 128]], axis=0)
        out = grad * ch[3:4, at : at + 128]
        chacc[3, :, at : at + 128] += fold(grad * raw)
        chacc[4, :, at : at + 128] += fold(grad)
        for d in (1, 2, 3):
            moved = pltpu.roll(ext, Q + 8 - d, 0)[:Q] * masks[d - 1]
            out = out + moved * ch[3 - d : 4 - d, at : at + 128]
            chacc[3 - d, :, at : at + 128] += fold(moved * raw)
        halo[:, at : at + 128] = grad[:8]
        return out

    pre_b = pre[0, :, inner : inner + 128]
    pre_c = pre[0, :, inner + 128 : inner + 256]
    sig_b, sig_c = sigmoid(pre_b), sigmoid(pre_c)
    b_rows, c_rows = pre_b * sig_b, pre_c * sig_c
    b_low, c_low = b_rows.astype(BF16), c_rows.astype(BF16)
    c_t = c_rows.T.astype(BF16)
    upper = lanes >= rows
    scores = jnp.where(upper, nt(b_low, c_low), 0.0)
    dlow = dstate[...].astype(BF16)
    dsb_all = mm(b_low, dlow)
    dscores = jnp.zeros((Q, Q), F32)
    sums = jnp.zeros((6 * Q, 128), F32)
    keep = jnp.zeros((8, 128), F32)
    for p in range(pairs):
        at = p * 128
        one = pj[0, :, p * 256 : p * 256 + 128].astype(F32)
        two = pj[0, :, p * 256 + 128 : p * 256 + 256].astype(F32)
        z = jnp.where(low, one, pltpu.roll(two, 64, 1))
        v = jnp.where(low, pltpu.roll(one, 64, 1), two)
        pr = pre[0, :, at : at + 128]
        sp = sigmoid(pr)
        xc = pr * sp
        l0 = jnp.broadcast_to(level[:, 2 * p : 2 * p + 1], (Q, Q))
        l1 = jnp.broadcast_to(level[:, 2 * p + 1 : 2 * p + 2], (Q, Q))
        le = jnp.where(low, l0, l1)
        dte = jnp.where(low, dt[:, 2 * p : 2 * p + 1], dt[:, 2 * p + 1 : 2 * p + 2])
        u = xc * dte
        skip = ch[5:6, at : at + 128]
        part = ys[0, :, at : at + 128]
        y = part + skip * xc
        sz = sigmoid(z)
        silz = z * sz
        gated = y * silz
        graw = sg[0, :, at : at + 128].astype(F32)
        scaled_rho = graw * rho
        scaled = gated * rho * ch[6:7, at : at + 128]
        sct[at : at + 128, :] = scaled.T.astype(BF16)
        scl[0, :, at : at + 128] = scaled.astype(BF16)
        gg = scaled_rho * ch[6:7, at : at + 128] - k2 * gated
        dy = gg * silz
        dz = gg * y * (sz + silz * (1.0 - sz))
        ulow = u.astype(BF16)
        dylow = dy.astype(BF16)
        w0 = jnp.exp2(jnp.minimum(level_t[2 * p : 2 * p + 1, :] - l0, 0.0))
        w1 = jnp.exp2(jnp.minimum(level_t[2 * p + 1 : 2 * p + 2, :] - l1, 0.0))
        wide = jnp.concatenate([(w0 * scores).astype(BF16), (w1 * scores).astype(BF16)], axis=1)
        dyb = jnp.concatenate(
            [jnp.where(low, dy, 0.0).astype(BF16), jnp.where(low, 0.0, dy).astype(BF16)], axis=0
        )
        ub = jnp.concatenate(
            [jnp.where(low, u, 0.0).astype(BF16), jnp.where(low, 0.0, u).astype(BF16)], axis=0
        )
        duw = mm(wide, dyb)
        gt = nt(ub, dylow)
        dscores = dscores + w0 * gt[:Q] + w1 * gt[Q:]
        last = le[Q - 1 : Q, :]
        lve = jnp.exp2(last - le)
        edy = (dy * jnp.exp2(le)).astype(BF16)
        ul = (u * lve).astype(BF16)
        edy_all[:, at : at + 128] = edy
        ul_all[:, at : at + 128] = ul
        dsb = dsb_all[:, at : at + 128]
        du = duw + lve * dsb
        r1 = dylow.astype(F32) * part - ulow.astype(F32) * duw
        r2 = ul.astype(F32) * dsb
        r1h, r2h = r1.astype(BF16), r2.astype(BF16)
        stacked = jnp.concatenate(
            [
                r1h,
                (r1 - r1h.astype(F32)).astype(BF16),
                r2h,
                (r2 - r2h.astype(F32)).astype(BF16),
                (dy * xc).astype(BF16),
                (du * xc).astype(BF16),
            ],
            axis=0,
        )
        sums = sums + mm(stacked, sel[p])
        decay = jnp.exp2(last)
        kept = fold(dlow[:, at : at + 128].astype(F32) * st[0, 0, :, at : at + 128].astype(F32)) * decay
        kept_high = kept.astype(BF16)
        keep = keep + mm(kept_high, sel[p]) + mm((kept - kept_high.astype(F32)).astype(BF16), sel[p])
        dstate[:, at : at + 128] = dstate[:, at : at + 128] * decay + mm(c_t, edy)
        dv = conv_back((du * dte + skip * dy) * (sp + xc * (1.0 - sp)), v, at)
        pg[0, :, p * 256 : p * 256 + 128] = jnp.where(low, dz, pltpu.roll(dv, 64, 1)).astype(BF16)
        pg[0, :, p * 256 + 128 : p * 256 + 256] = jnp.where(low, pltpu.roll(dz, 64, 1), dv).astype(BF16)
    dsc = jnp.where(upper, dscores, 0.0)
    db = mm(dsc.astype(BF16), c_low) + nt(ul_all[...], dlow)
    dc = mm(dsc.T.astype(BF16), b_low) + nt(edy_all[...], st[0, 0])
    raw_b = pj[0, :, width : width + 128].astype(F32)
    raw_c = pj[0, :, width + 128 : width + 256].astype(F32)
    pg[0, :, width : width + 128] = conv_back(
        db * (sig_b + b_rows * (1.0 - sig_b)), raw_b, inner
    ).astype(BF16)
    pg[0, :, width + 128 : width + 256] = conv_back(
        dc * (sig_c + c_rows * (1.0 - sig_c)), raw_c, inner + 128
    ).astype(BF16)
    r1 = sums[:Q] + sums[Q : 2 * Q]
    r2 = sums[2 * Q : 3 * Q] + sums[3 * Q : 4 * Q]
    da = (
        jnp.dot(upper.astype(F32), r1, precision=EXACT, preferred_element_type=F32)
        + jnp.dot((rows > lanes).astype(F32), r2, precision=EXACT, preferred_element_type=F32)
        + jnp.sum(keep, axis=0, keepdims=True)
    )
    ddt = da * hp[2:3, :] + sums[5 * Q :]
    ds = ddt * sigmoid(arg)
    pg[0, :, width + 256 : width + 384] = ds.astype(BF16)
    hacc[0] += fold(ds)
    hacc[1] += fold(da * dt)
    hacc[2] += fold(sums[4 * Q : 5 * Q])


def mix_backward(pj, marks, rk, sg, pre, ys, st, hp, ch, sel):
    seqs, length, total = pj.shape
    width = total - 384
    inner = width // 2
    pairs = inner // 128
    chunks = length // Q

    def row(n):
        return pl.BlockSpec((1, Q, n), lambda s, c: (s, chunks - 1 - c, 0))

    def whole(shape):
        return pl.BlockSpec(shape, lambda s, c: (0,) * len(shape))

    return pl.pallas_call(
        functools.partial(bwd_kernel, pairs),
        grid=(seqs, chunks),
        in_specs=[
            row(total),
            pl.BlockSpec((1, 8, Q), lambda s, c: (s, 0, chunks - 1 - c)),
            pl.BlockSpec((1, 8, Q), lambda s, c: (s, 0, chunks - 1 - c)),
            row(inner),
            row(inner + 256),
            row(inner),
            pl.BlockSpec((1, 1, 128, inner), lambda s, c: (s, chunks - 1 - c, 0, 0)),
            whole(hp.shape),
            whole(ch.shape),
            whole(sel.shape),
        ],
        out_specs=[
            row(total),
            whole((5, 8, inner + 256)),
            whole((3, 8, 128)),
            pl.BlockSpec((inner, Q), lambda s, c: (0, s * chunks + chunks - 1 - c)),
            row(inner),
        ],
        out_shape=[
            jax.ShapeDtypeStruct((seqs, length, total), BF16),
            jax.ShapeDtypeStruct((5, 8, inner + 256), F32),
            jax.ShapeDtypeStruct((3, 8, 128), F32),
            jax.ShapeDtypeStruct((inner, seqs * length), BF16),
            jax.ShapeDtypeStruct((seqs, length, inner), BF16),
        ],
        scratch_shapes=[
            pltpu.VMEM((128, inner), F32),
            pltpu.VMEM((8, inner + 256), F32),
            pltpu.VMEM((Q, inner), BF16),
            pltpu.VMEM((Q, inner), BF16),
        ],
        compiler_params=pltpu.CompilerParams(vmem_limit_bytes=60 * 2**20),
        name="mix_backward",
    )(pj, marks, rk, sg, pre, ys, st, hp, ch, sel)


def marks_kernel(seg, marks):
    seqs, length = seg.shape
    ids = seg[...].astype(F32)
    lane = lax.broadcasted_iota(jnp.int32, (seqs, length), 1)
    back = [
        jnp.where((pltpu.roll(ids, d, 1) == ids) & (lane >= d), 1.0, 0.0) for d in (1, 2, 3)
    ]
    ahead = [
        jnp.where((pltpu.roll(ids, length - d, 1) == ids) & (lane < length - d), 1.0, 0.0)
        for d in (1, 2, 3)
    ]
    before = [ids[:, 0:1]] + [ids[:, at - 1 : at] for at in range(Q, length, Q)]
    level = jnp.concatenate(
        [-RESET * (ids[:, n * Q : (n + 1) * Q] - b) for n, b in enumerate(before)], axis=1
    )
    all_rows = [*back, level, *ahead, jnp.zeros((seqs, length), F32)]
    for n in range(seqs):
        marks[n] = jnp.concatenate([r[n : n + 1, :] for r in all_rows], axis=0)


def marks_of(seg):
    return pl.pallas_call(
        marks_kernel,
        out_shape=jax.ShapeDtypeStruct((seg.shape[0], 8, seg.shape[1]), F32),
        name="marks",
    )(seg)


def selectors(pairs):
    lane = lax.broadcasted_iota(jnp.int32, (pairs, 128, 128), 1)
    pair = lax.broadcasted_iota(jnp.int32, (pairs, 128, 128), 0)
    out = lax.broadcasted_iota(jnp.int32, (pairs, 128, 128), 2)
    return (out == 2 * pair + lane // 64).astype(BF16)


def norm_kernel(wide, red, rk, got, ssem, rsem):
    d = lax.axis_index("dp")
    s = lax.axis_index("seq")
    groups = got.shape[0]
    bar = pltpu.get_barrier_semaphore()
    for j in range(1, groups):
        pl.semaphore_signal(bar, inc=1, device_id=(d, lax.rem(s + j, groups)), device_id_type=MESH)
    pl.semaphore_wait(bar, groups - 1)
    sends = [
        pltpu.make_async_remote_copy(
            src_ref=red, dst_ref=got.at[j], send_sem=ssem.at[j], recv_sem=rsem.at[j],
            device_id=(d, lax.rem(s + j, groups)), device_id_type=MESH,
        )
        for j in range(1, groups)
    ]
    for copy in sends:
        copy.start()
    total = red[...]
    for j, copy in enumerate(sends):
        copy.wait()
        total = total + got[j + 1]
    rho = lax.rsqrt(total[:, 0:1] / wide + EPSILON)
    rk[...] = jnp.concatenate(
        [rho, rho * rho * rho * total[:, 1:2] / wide, jnp.zeros_like(total[:, 2:])], axis=1
    )


def norms(red, wide, groups):
    vmem = pl.BlockSpec(memory_space=pltpu.VMEM)
    return pl.pallas_call(
        functools.partial(norm_kernel, wide),
        in_specs=[vmem],
        out_specs=vmem,
        out_shape=jax.ShapeDtypeStruct(red.shape, F32),
        scratch_shapes=[
            pltpu.VMEM((groups, *red.shape), F32),
            pltpu.SemaphoreType.DMA((groups,)),
            pltpu.SemaphoreType.DMA((groups,)),
        ],
        compiler_params=pltpu.CompilerParams(collective_id=3, has_side_effects=True),
        name="norms",
    )(red)


def final_kernel(
    groups, span, mine, share, gw, w_in, wog, w_out, osum, ngrad, tok, cot, gains, sums,
    res, tgrad, wig, wgr, nsum, gsum, chan, head,
):
    @pl.when(pl.program_id(0) == 0)
    def _():
        inner = span // 2
        shared = sums[0, :, inner:]
        heads = sums[0, :, :128]
        for g in range(1, groups):
            shared = shared + sums[g, :, inner:]
            heads = heads + pltpu.roll(sums[g, :, :128], g * mine, 1)
        row = jnp.concatenate([*[sums[g, :, :inner] for g in range(groups)], shared], axis=1)
        first = lax.axis_index("dp") * share
        own = pltpu.roll(row, row.shape[1] - first, 1)[:, : chan.shape[0]]
        chan[...] = own.T
        head[...] = heads

    total = jnp.zeros((w_in.shape[0], 1), F32)
    for g in range(groups):
        here = slice(g * span, (g + 1) * span)
        grad = gw[g, :, :span].astype(F32)
        wig[:, here] = grad
        total = total + jnp.sum(grad * w_in[:, here].astype(F32), axis=1, keepdims=True)
    at = groups * span
    width = gw.shape[2] - 128
    shared = gw[0, :, span:width].astype(F32)
    steps = gw[0, :, width:].astype(F32)
    for g in range(1, groups):
        shared = shared + gw[g, :, span:width].astype(F32)
        steps = steps + pltpu.roll(gw[g, :, width:].astype(F32), g * mine, 1)
    mid = at + width - span
    wig[:, at:mid] = shared
    wig[:, mid:] = steps[:, : groups * mine]
    total = total + jnp.sum(shared * w_in[:, at:mid].astype(F32), axis=1, keepdims=True)
    total = total + jnp.sum(
        steps[:, : groups * mine] * w_in[:, mid:].astype(F32), axis=1, keepdims=True
    )
    nsum[...] = jnp.broadcast_to(total, nsum.shape)
    grad = wog[...].astype(F32)
    wgr[...] = grad
    gsum[...] = jnp.broadcast_to(
        jnp.sum(grad * w_out[...].astype(F32), axis=1, keepdims=True), gsum.shape
    )
    x = tok[...].astype(F32)
    res[...] = (x + osum[...].astype(F32)).astype(BF16)
    inverse = lax.rsqrt(jnp.mean(x * x, axis=1, keepdims=True) + EPSILON)
    unit = x * inverse
    grad = ngrad[...].astype(F32) * gains[0:1, :]
    tgrad[...] = cot[...].astype(F32) + inverse * (
        grad - unit * jnp.mean(grad * unit, axis=1, keepdims=True)
    )


def final(gw, w_in, wog, w_out, osum, ngrad, tok, cot, gains, sums, span, mine, share):
    groups, rows, total = gw.shape
    steps = next(n for n in (4, 2, 1) if rows % (16 * n) == 0)

    def part(a):
        return pl.BlockSpec((a.shape[0] // steps, a.shape[1]), lambda i: (i, 0))

    tall = [w_in, wog, w_out, osum, ngrad, tok, cot]
    shapes = [
        (tok.shape, BF16), (tok.shape, F32), (w_in.shape, F32), (wog.shape, F32),
        ((rows, 128), F32), ((wog.shape[0], 128), F32),
    ]
    outs = [jax.ShapeDtypeStruct(*n) for n in shapes]
    chan = jax.ShapeDtypeStruct((-(-share // 128) * 128, 8), F32)
    head = jax.ShapeDtypeStruct((8, 128), F32)
    return pl.pallas_call(
        functools.partial(final_kernel, groups, span, mine, share),
        grid=(steps,),
        in_specs=[
            pl.BlockSpec((groups, rows // steps, total), lambda i: (0, i, 0)),
            *[part(a) for a in tall],
            pl.BlockSpec(gains.shape, lambda i: (0, 0)),
            pl.BlockSpec(sums.shape, lambda i: (0, 0, 0)),
        ],
        out_specs=[
            *[part(o) for o in outs],
            pl.BlockSpec(chan.shape, lambda i: (0, 0)),
            pl.BlockSpec(head.shape, lambda i: (0, 0)),
        ],
        out_shape=[*outs, chan, head],
        compiler_params=pltpu.CompilerParams(vmem_limit_bytes=60 * 2**20),
        name="final",
    )(gw, *tall, gains, sums)


def gather_kernel(
    dims, w_in, dt_in, wo_in, small_in, tok_in, cot_in,
    turned_o, cot_o, pj_o, sg_o, w_o, wo_o, small_o,
    tok, cot, wbig, wo, small, pjv, sgv, turned,
    szu, szd, rz, sy, ry, wsu, wsd, wrz, wsy, wry, bx_s, bx_r, bc_s, bc_r, loc, out,
):
    deep, pieces, rows, inner, part, length, groups = dims
    d = lax.axis_index("dp")
    s = lax.axis_index("seq")
    z = d // 2
    y = d % 2
    top = deep - 1
    up, down, side = (d + 2, s), (d - 2, s), (d + 1 - 2 * y, s)
    across, twin = (d, s + 2 - 4 * (s // 2)), (d, s + 1 - 2 * (s % 2))
    opposite = across[1]

    bar = pltpu.get_barrier_semaphore()

    @pl.when(z < top)
    def _():
        pl.semaphore_signal(bar, inc=1, device_id=up, device_id_type=MESH)

    @pl.when(z > 0)
    def _():
        pl.semaphore_signal(bar, inc=1, device_id=down, device_id_type=MESH)

    for who in (side, across, twin):
        pl.semaphore_signal(bar, inc=1, device_id=who, device_id_type=MESH)
    pl.semaphore_wait(bar, 3 + jnp.minimum(z, 1) + jnp.minimum(top - z, 1))

    def send(src, dst, ssem, rsem, who):
        return pltpu.make_async_remote_copy(
            src_ref=src, dst_ref=dst, send_sem=ssem, recv_sem=rsem,
            device_id=who, device_id_type=MESH,
        )

    width = 2 * inner

    def cols(k):
        return pl.ds(width + 256, 128) if k == 1 else pl.ds(width if k == 2 else (k - 3) * 256, 256)

    def held(k, owner):
        if k == 0:
            return small.at[owner]
        return wbig.at[pl.ds(pl.multiple_of(owner * rows, 16), rows), cols(k)]

    def source(k):
        if k == 0:
            return small_in.at[...]
        if k == 1:
            return dt_in.at[...]
        if k == 2:
            return w_in.at[:, pl.ds(width * groups, 256)]
        return w_in.at[:, pl.ds(pl.multiple_of(s * width + (k - 3) * 256, 128), 256)]

    def own_send(k):
        src, dst = source(k), held(k, d)

        @pl.when(z < top)
        def _():
            send(src, dst, szu.at[k, z], rz.at[k, z], up).start()

        @pl.when(z > 0)
        def _():
            send(src, dst, szd.at[k, z], rz.at[k, z], down).start()

        send(src, dst, sy.at[k, z], ry.at[k, z], side).start()

    def hop(k, h):
        below, above = z - h, z + h

        @pl.when(below >= 0)
        def _():
            ref = held(k, below * 2 + y)
            send(ref, ref, szu.at[k, below], rz.at[k, below], up).wait_recv()

            @pl.when(z < top)
            def _():
                send(ref, ref, szu.at[k, below], rz.at[k, below], up).start()

            send(ref, ref, sy.at[k, below], ry.at[k, below], side).start()

        @pl.when(above <= top)
        def _():
            ref = held(k, above * 2 + y)
            send(ref, ref, szd.at[k, above], rz.at[k, above], down).wait_recv()

            @pl.when(z > 0)
            def _():
                send(ref, ref, szd.at[k, above], rz.at[k, above], down).start()

            send(ref, ref, sy.at[k, above], ry.at[k, above], side).start()

    def arrive(k):
        for e in range(deep):
            ref = held(k, e * 2 + 1 - y)
            send(ref, ref, sy.at[k, e], ry.at[k, e], side).wait_recv()

    def own_copy(src, dst, sem):
        return pltpu.make_async_copy(src, dst, sem)

    here = pl.multiple_of(s * part, 16)
    there = pl.multiple_of(opposite * part, 16)
    locals_ = [
        own_copy(small_in, small.at[d], loc.at[0]),
        own_copy(
            w_in.at[:, pl.ds(pl.multiple_of(s * width, 128), width)],
            wbig.at[pl.ds(pl.multiple_of(d * rows, 16), rows), pl.ds(0, width)],
            loc.at[1],
        ),
    ]
    for q in range(2):
        locals_.append(own_copy(tok_in.at[q], tok.at[q, pl.ds(here, part)], loc.at[2 + q]))
        locals_.append(own_copy(cot_in.at[q], cot.at[q, pl.ds(here, part)], loc.at[4 + q]))
    for k in (1, 2):
        locals_.append(own_copy(source(k), held(k, d), loc.at[6 + k]))
    half = wo_in.shape[0]
    mine = z == s

    def root_copy():
        return own_copy(wo_in, wo.at[pl.ds(pl.multiple_of(y * half, 16), half)], loc.at[6])

    def block_sends(which, src, dst, q):
        spot = dst.at[q, pl.ds(here, part)]
        i = which * 2 + q
        send(src.at[q], spot, bx_s.at[i], bx_r.at[i], across).start()
        send(src.at[q], spot, bc_s.at[0, i], bc_r.at[0, i], twin).start()

    def block_forward(which, dst, q):
        spot = dst.at[q, pl.ds(there, part)]
        i = which * 2 + q
        send(spot, spot, bx_s.at[i], bx_r.at[i], across).wait_recv()
        send(spot, spot, bc_s.at[1, i], bc_r.at[1, i], twin).start()

    def block_arrive(which, dst, q):
        i = which * 2 + q
        for n in range(2):
            spot = dst.at[q, pl.ds(here, part)]
            send(spot, spot, bc_s.at[n, i], bc_r.at[n, i], twin).wait_recv()

    lump = half // LUMPS

    def wo_piece(i, col):
        m = col * LUMPS + i
        return m, wo.at[pl.ds(pl.multiple_of(m * lump, 16), lump)]

    def wo_send(i, src=None):
        m, ref = wo_piece(i, y)
        src = ref if src is None else src

        @pl.when((z >= s) & (z < top))
        def _():
            send(src, ref, wsu.at[m], wrz.at[m], up).start()

        @pl.when((z <= s) & (z > 0))
        def _():
            send(src, ref, wsd.at[m], wrz.at[m], down).start()

        send(src, ref, wsy.at[m], wry.at[m], side).start()

    def wo_root(i):
        @pl.when(mine)
        def _():
            wo_send(i, wo_in.at[pl.ds(i * lump, lump)])

    def wo_hop(i, h):
        @pl.when((z - s == h) | (s - z == h))
        def _():
            m, ref = wo_piece(i, y)
            send(ref, ref, wsu.at[m], wrz.at[m], up).wait_recv()
            wo_send(i)

    def wo_arrive(i):
        m, ref = wo_piece(i, 1 - y)
        send(ref, ref, wsy.at[m], wry.at[m], side).wait_recv()

    tile = 256
    long = 512

    def project(k):
        c = pl.ds(width, 384) if k == 2 else cols(k)

        def step(i, _):
            q, r = i // (length // long), i % (length // long)
            at = pl.ds(pl.multiple_of(r * long, long), long)
            pjv[q, at, c] = mm(tok[q, at, :], wbig[:, c]).astype(BF16)
            return 0

        lax.fori_loop(0, 2 * length // long, step, 0)
        own_copy(pjv.at[:, :, c], pj_o.at[:, :, c], out.at[k]).start()

    for c in locals_:
        c.start()

    @pl.when(mine)
    def _():
        root_copy().start()

    for q in range(2):
        block_sends(0, tok_in, tok, q)
    ahead = 3
    for k in range(ahead):
        own_send(k)
    done = []

    def hops(t):
        for h in range(1, deep):
            if 0 <= t - h < pieces:
                hop(t - h, h)
        for h in range(1, deep):
            if 0 <= t - h - WOFF < LUMPS:
                wo_hop(t - h - WOFF, h)
        if 0 <= t - WOFF < LUMPS:
            wo_root(t - WOFF)
        if ahead <= t + ahead - 1 < pieces:
            own_send(t + ahead - 1)

    steps = max(pieces, WOFF + LUMPS) + deep - 1
    count = dict(next=1)

    def ready(n):
        for _ in range(n):
            if count["next"] < pieces:
                arrive(count["next"])
                if count["next"] > 1:
                    project(count["next"])
                count["next"] += 1

    share = tok.shape[2] // (2 * deep)

    def norm_step(i, _):
        q, r = i // (length // 64), i % (length // 64)
        at = pl.multiple_of(r * 64, 64)
        x = tok[q, pl.ds(at, 64), :].astype(F32)
        inv = lax.rsqrt(jnp.mean(x * x, axis=1, keepdims=True) + EPSILON)
        gains = jnp.concatenate([small[e, 0:1, :share] for e in range(2 * deep)], axis=1)
        tok[q, pl.ds(at, 64), :] = (x * inv * gains.astype(F32)).astype(BF16)
        return 0

    def turn_step(i, _):
        q, r = i // (length // tile), i % (length // tile)
        at = pl.multiple_of(r * tile, tile)
        to = pl.multiple_of(i * tile, tile)
        for j in range(0, tok.shape[2], 128):
            turned[j : j + 128, pl.ds(to, tile)] = tok[q, pl.ds(at, tile), j : j + 128].T
        return 0

    def grad_step(i, _):
        q, r = i // (length // long), i % (length // long)
        at = pl.ds(pl.multiple_of(r * long, long), long)
        sgv[q, at, :] = nt(cot[q, at, :], wo[...]).astype(BF16)
        return 0

    for t in range(1, steps):
        hops(t)
        if t == 3:
            block_forward(0, tok, 0)
        if t == 6:
            block_forward(0, tok, 1)
            for q in range(2):
                block_sends(1, cot_in, cot, q)
        if t == 7:
            for i in (0, 1, 2, 4, 6, 7):
                locals_[i].wait()
            block_arrive(0, tok, 0)
            block_arrive(0, tok, 1)
            for q in range(2):
                spot = tok.at[q, pl.ds(there, part)]
                send(spot, spot, bc_s.at[1, q], bc_r.at[1, q], twin).wait_send()
            arrive(0)
            own_copy(small, small_o, out.at[0]).start()
            lax.fori_loop(0, 2 * length // 64, norm_step, 0)
            lax.fori_loop(0, 2 * length // tile, turn_step, 0)
            own_copy(turned, turned_o, out.at[pieces]).start()
        if t == 10:
            block_forward(1, cot, 0)
        if t == 11:
            block_forward(1, cot, 1)
        if t > 7:
            ready(2 if t == 8 else 1)

    @pl.when(mine)
    def _():
        root_copy().wait()

    locals_[3].wait()
    locals_[5].wait()
    for i in range(LUMPS):
        wo_arrive(i)
    own_copy(wo, wo_o, out.at[pieces + 2]).start()
    block_arrive(1, cot, 0)
    block_arrive(1, cot, 1)
    own_copy(cot, cot_o, out.at[pieces + 3]).start()
    lax.fori_loop(0, 2 * length // long, grad_step, 0)
    own_copy(sgv, sg_o, out.at[pieces + 4]).start()
    ready(pieces)
    own_copy(wbig, w_o, out.at[pieces + 1]).start()
    for k in range(pieces):
        for e in range(deep):
            ref = held(k, e * 2 + y)

            @pl.when((z >= e) & (z < top))
            def _():
                send(ref, ref, szu.at[k, e], rz.at[k, e], up).wait_send()

            @pl.when((z <= e) & (z > 0))
            def _():
                send(ref, ref, szd.at[k, e], rz.at[k, e], down).wait_send()

            send(ref, ref, sy.at[k, e], ry.at[k, e], side).wait_send()
    for i in range(LUMPS):
        m, ref = wo_piece(i, y)

        @pl.when((z >= s) & (z < top))
        def _():
            send(ref, ref, wsu.at[m], wrz.at[m], up).wait_send()

        @pl.when((z <= s) & (z > 0))
        def _():
            send(ref, ref, wsd.at[m], wrz.at[m], down).wait_send()

        send(ref, ref, wsy.at[m], wry.at[m], side).wait_send()
    for which, dst in ((0, tok), (1, cot)):
        for q in range(2):
            i = which * 2 + q
            spot = dst.at[q, pl.ds(here, part)]
            send(spot, spot, bx_s.at[i], bx_r.at[i], across).wait_send()
            for n in range(1 + which):
                send(spot, spot, bc_s.at[n, i], bc_r.at[n, i], twin).wait_send()
    own_copy(small, small_o, out.at[0]).wait()
    for k in range(2, pieces):
        c = pl.ds(width, 384) if k == 2 else cols(k)
        own_copy(pjv.at[:, :, c], pj_o.at[:, :, c], out.at[k]).wait()
    own_copy(turned, turned_o, out.at[pieces]).wait()
    own_copy(wbig, w_o, out.at[pieces + 1]).wait()
    own_copy(wo, wo_o, out.at[pieces + 2]).wait()
    own_copy(cot, cot_o, out.at[pieces + 3]).wait()
    own_copy(sgv, sg_o, out.at[pieces + 4]).wait()


def gather(w_in, dt_in, w_out, small, tokens, cotangent, inner, shards, groups):
    rows = w_in.shape[0]
    total = 2 * inner + 384
    seqs, part, model = tokens.shape
    length = part * groups
    deep = shards // 2
    pieces = inner // 128 + 3
    any_ = pl.BlockSpec(memory_space=pl.ANY)
    dma = pltpu.SemaphoreType.DMA
    small_rows, small_cols = small.shape
    full = (shards * rows, total)
    shapes = [
        (model, seqs * length), (seqs, length, model), (seqs, length, total), (seqs, length, inner),
        full, (inner, model), (shards, small_rows, small_cols),
    ]
    return pl.pallas_call(
        functools.partial(gather_kernel, (deep, pieces, rows, inner, part, length, groups)),
        in_specs=[any_] * 6,
        out_specs=[any_] * 7,
        out_shape=[jax.ShapeDtypeStruct(n, BF16) for n in shapes],
        scratch_shapes=[
            pltpu.VMEM(shapes[1], BF16),
            pltpu.VMEM(shapes[1], BF16),
            pltpu.VMEM(full, BF16),
            pltpu.VMEM((inner, model), BF16),
            pltpu.VMEM(shapes[6], BF16),
            pltpu.VMEM(shapes[2], BF16),
            pltpu.VMEM(shapes[3], BF16),
            pltpu.VMEM(shapes[0], BF16),
            dma((pieces, deep)), dma((pieces, deep)), dma((pieces, deep)),
            dma((pieces, deep)), dma((pieces, deep)),
            *[dma((2 * LUMPS,))] * 5,
            dma((4,)), dma((4,)), dma((2, 4)), dma((2, 4)),
            dma((9,)), dma((pieces + 5,)),
        ],
        compiler_params=pltpu.CompilerParams(
            collective_id=1, has_side_effects=True, vmem_limit_bytes=56 * 2**20
        ),
        name="gather_project",
    )(w_in, dt_in, w_out, small, tokens, cotangent)


def greet(z, y, s, deep, others):
    bar = pltpu.get_barrier_semaphore()
    for e in range(deep):
        @pl.when(z != e)
        def _():
            pl.semaphore_signal(bar, inc=1, device_id=(2 * e + y, s), device_id_type=MESH)

    for who in others:
        pl.semaphore_signal(bar, inc=1, device_id=who, device_id_type=MESH)
    pl.semaphore_wait(bar, len(others) + deep - 1)


def send(src, dst, ssem, rsem, who):
    return pltpu.make_async_remote_copy(
        src_ref=src, dst_ref=dst, send_sem=ssem, recv_sem=rsem, device_id=who, device_id_type=MESH
    )


def add_into(dst, src):
    count = dst.shape[0]
    some = next(n for n in (64, 48, 32, 16) if count % n == 0)

    def step(i, _):
        at = pl.ds(pl.multiple_of(i * some, 16), some)
        dst[at, :] = (dst[at, :].astype(F32) + src[at, :].astype(F32)).astype(BF16)
        return 0

    lax.fori_loop(0, count // some, step, 0)


CUTS = ((0, 512), (512, 512), (1536, 384), (1024, 256), (1280, 256))
PARTS = len(CUTS)


def scatter_kernel(
    dims, nt_in, pg_in, st_in, sc_in, cot_in, wo_in, wi_in, ch_in, he_in,
    gw_o, wo_o, out_o, ng_o, sm_o,
    nt_v, pg_v, st_v, sc_v, wo_v, cw, pv, yb, zb, tw, xr, stage, gw, ybw, zbw, ch_v, he_v,
    vec, vgot, vall,
    sy, ry, su, sd, rz, gx_s, gx_r, gc_s, gc_r, tw_s, tw_r, xr_s, xr_r,
    wy_s, wy_r, wu_s, wd_s, wz_r, bx_s, bx_r, bc_s, bc_r, v_s, v_r, loc, out,
):
    deep, rows, part, length = dims
    d = lax.axis_index("dp")
    s = lax.axis_index("seq")
    z = d // 2
    y = d % 2
    x = s // 2
    c = s % 2
    top = deep - 1
    model = wi_in.shape[0]
    up, down, side = (d + 2, s), (d - 2, s), (d + 1 - 2 * y, s)
    across, twin = (d, s + 2 - 4 * x), (d, s + 1 - 2 * c)
    greet(z, y, s, deep, (side, across, twin))

    def cut(k):
        return pl.ds(*CUTS[k])

    def lines(ref, i, count=rows):
        return ref.at[pl.ds(pl.multiple_of(i * count, 16), count)]

    cot_v = cw.at[:, pl.ds(0, model)]
    wi_v = cw.at[pl.ds(0, model), :]
    loads = dict(
        ch=pltpu.make_async_copy(ch_in, ch_v, loc.at[2]),
        he=pltpu.make_async_copy(he_in, he_v, loc.at[3]),
        st=pltpu.make_async_copy(st_in, st_v, loc.at[0]),
        cot=pltpu.make_async_copy(cot_in, cot_v, loc.at[1]),
        sc=pltpu.make_async_copy(sc_in, sc_v, loc.at[6]),
        wo=pltpu.make_async_copy(wo_in, wo_v, loc.at[7]),
        nt=pltpu.make_async_copy(nt_in, nt_v, loc.at[4]),
        pg=pltpu.make_async_copy(pg_in, pg_v, loc.at[5]),
    )
    for load in loads.values():
        load.start()
    load_wi = pltpu.make_async_copy(wi_in, wi_v, loc.at[8])

    def v_send(n, src, dst, who):
        return send(src, dst, v_s.at[n], v_r.at[n], who)

    def v_y():
        return v_send(0, vec, vgot.at[deep], side)

    def v_z(e):
        return send(vec, vgot.at[z], v_s.at[1 + e], v_r.at[1 + z], (2 * e + y, s))

    def v_from(e):
        return send(vec, vgot.at[e], v_s.at[1 + e], v_r.at[1 + e], (2 * e + y, s))

    def v_seq(n, owner, who):
        return v_send(1 + deep + n, vall.at[owner], vall.at[owner], who)

    def v_start():
        vec[...] = jnp.concatenate(
            [
                jnp.sum(ch_v[...], axis=1),
                jnp.concatenate(
                    [jnp.sum(he_v[...], axis=1), jnp.zeros((3, vec.shape[1] - 128), F32)], axis=1
                ),
            ],
            axis=0,
        )
        v_y().start()

    def v_sum():
        v_y().wait()
        vec[...] = vec[...] + vgot[deep]
        for e in range(deep):
            @pl.when(z != e)
            def _():
                v_z(e).start()

    def v_total():
        for e in range(deep):
            @pl.when(z != e)
            def _():
                v_z(e).wait_send()
                v_from(e).wait_recv()

            @pl.when(z == e)
            def _():
                vgot[e] = vec[...]

        total = vgot[0]
        for e in range(1, deep):
            total = total + vgot[e]
        vall[s] = total
        v_seq(0, s, across).start()
        v_seq(1, s, twin).start()

    def v_spread():
        v_seq(0, across[1], across).wait_recv()
        v_seq(2, across[1], twin).start()

    both = ((0, out_o), (1, ng_o))

    def twin_send(n, turn, q):
        return send(stage.at[q], tw.at[n, turn, q], tw_s.at[q], tw_r.at[n, turn, q], twin)

    def product(n, q, owner, j):
        at = pl.ds(pl.multiple_of(q * length + owner * part, 16), part)
        if n == 0:
            return mm(sc_v[at, :], wo_v[:, j : j + 512])
        return nt(pg_v[at, :], cw[j : j + 512, :])

    def exchange(n, turn):
        half = 1 - x if turn == 0 else x
        for q in range(2):
            if (n, turn) != (0, 0):
                twin_send(n, turn, q).wait_send()
            for j in range(0, model, 512):
                stage[q, :, j : j + 512] = product(n, q, 2 * half + 1 - c, j).astype(BF16)
            twin_send(n, turn, q).start()
        for q in range(2):
            twin_send(n, turn, q).wait_recv()
            for j in range(0, model, 512):
                tw[n, turn, q, :, j : j + 512] = (
                    tw[n, turn, q, :, j : j + 512].astype(F32) + product(n, q, 2 * half + c, j)
                ).astype(BF16)
            if turn == 0:
                x_send(n, q).start()

    def x_send(n, q):
        return send(tw.at[n, 0, q], xr.at[n, q], xr_s.at[n, q], xr_r.at[n, q], across)

    def x_finish(n, dst):
        for q in range(2):
            x_send(n, q).wait_recv()
            add_into(xr.at[n, q], tw.at[n, 1, q])
            pltpu.make_async_copy(xr.at[n, q], dst.at[q], out.at[2 + 2 * n + q]).start()

    def weigh(k):
        def step(i, _):
            at = pl.ds(pl.multiple_of(i * rows, 16), rows)
            pv[at, cut(k)] = mm(nt_v[at, :], pg_v[:, cut(k)]).astype(BF16)
            return 0

        lax.fori_loop(0, 2 * deep, step, 0)

    def block(e, k):
        return pv.at[pl.ds(pl.multiple_of((2 * e + y) * rows, 16), rows), cut(k)]

    def y_send(k, e):
        src = pv.at[pl.ds(pl.multiple_of((2 * e + 1 - y) * rows, 16), rows), cut(k)]
        return send(src, lines(yb, e).at[:, cut(k)], sy.at[k, e], ry.at[k, e], side)

    def y_start(k):
        for e in range(deep):
            y_send(k, e).start()

    def y_add(k):
        for e in range(deep):
            y_send(k, e).wait_recv()
            add_into(block(e, k), lines(yb, e).at[:, cut(k)])

    def z_send(k, e, slot, sem, who):
        return send(block(e, k), lines(zb, slot).at[:, cut(k)], sem.at[k, e], rz.at[k, slot], who)

    def hop(k, h):
        @pl.when(z == h - 1)
        def _():
            for e in range(top, h - 1, -1):
                if h > 1:
                    z_send(k, e, e, su, up).wait_recv()
                    add_into(block(e, k), lines(zb, e).at[:, cut(k)])
                z_send(k, e, e, su, up).start()

        @pl.when(z == deep - h)
        def _():
            for e in range(deep - h):
                if h > 1:
                    z_send(k, e, e, sd, down).wait_recv()
                    add_into(block(e, k), lines(zb, e).at[:, cut(k)])
                z_send(k, e, deep if e == deep - h - 1 else e, sd, down).start()

    def g_spot(who, k):
        return gw_o.at[who, :, cut(k)]

    def finish(k):
        mine = block(z, k)

        @pl.when(z > 0)
        def _():
            z_send(k, z, z, su, up).wait_recv()
            add_into(mine, lines(zb, z).at[:, cut(k)])

        @pl.when(z < top)
        def _():
            z_send(k, z, deep, sd, down).wait_recv()
            add_into(mine, lines(zb, deep).at[:, cut(k)])

        send(mine, g_spot(s, k), gx_s.at[k], gx_r.at[k], across).start()
        send(mine, g_spot(s, k), gc_s.at[0, k], gc_r.at[0, k], twin).start()
        pltpu.make_async_copy(mine, g_spot(s, k), loc.at[9 + k]).start()

    def spread(k):
        spot = g_spot(across[1], k)
        send(spot, spot, gx_s.at[k], gx_r.at[k], across).wait_recv()
        send(spot, spot, gc_s.at[1, k], gc_r.at[1, k], twin).start()

    half = gw.shape[0] // 2
    lump = half // LUMPS

    def w_rows(col, i):
        return gw.at[pl.ds(pl.multiple_of(col * half + i * lump, 16), lump)]

    def piece(ref, i):
        return ref.at[pl.ds(i * lump, lump)]

    def wy_send(i):
        return send(w_rows(1 - y, i), piece(ybw, i), wy_s.at[i], wy_r.at[i], side)

    def w_compute():
        tall = 2 * lump
        for n in range(LUMPS):
            col, i = (1 - y, n) if n < LUMPS // 2 else (y, n - LUMPS // 2)
            at = pl.ds(pl.multiple_of(col * half + i * tall, 16), tall)
            for j in range(0, model, 512):
                gw[at, j : j + 512] = mm(st_v[at, :], cw[:, j : j + 512]).astype(BF16)
            if n < LUMPS // 2:
                wy_send(2 * i).start()
                wy_send(2 * i + 1).start()

    def from_below(i):
        return send(w_rows(y, i), piece(zbw.at[0], i), wu_s.at[i], wz_r.at[0, i], up)

    def from_above(i):
        return send(w_rows(y, i), piece(zbw.at[1], i), wd_s.at[i], wz_r.at[1, i], down)

    def w_cast(i, who, ssem, rsem):
        return send(piece(wo_o, i), piece(wo_o, i), ssem.at[i], rsem.at[i], who)

    def w_root(i, who, ssem, rsem):
        return send(w_rows(y, i), piece(wo_o, i), ssem.at[i], rsem.at[i], who)

    def w_keep(i):
        return pltpu.make_async_copy(w_rows(y, i), piece(wo_o, i), loc.at[9 + PARTS + i])

    root = z == s

    def w_chain(i, h):
        last = h == deep - 1
        below = root & (z > 0) if last else (z < s) & (z == h) & (h > 0)
        above = root & (z < top) if last else (z > s) & (top - z == h) & (h > 0)

        @pl.when(root if last else ((z < s) & (z == h)) | ((z > s) & (top - z == h)))
        def _():
            wy_send(i).wait_recv()
            add_into(w_rows(y, i), piece(ybw, i))

        @pl.when(below)
        def _():
            from_below(i).wait_recv()
            add_into(w_rows(y, i), piece(zbw.at[0], i))

        @pl.when(above)
        def _():
            from_above(i).wait_recv()
            add_into(w_rows(y, i), piece(zbw.at[1], i))

        if last:

            @pl.when(root)
            def _():
                w_keep(i).start()
                w_root(i, across, bx_s, bx_r).start()
                w_root(i, twin, bc_s, bc_r).start()

        else:

            @pl.when((z < s) & (z == h))
            def _():
                from_below(i).start()

            @pl.when((z > s) & (top - z == h))
            def _():
                from_above(i).start()

    def w_spread(i):
        @pl.when(across[1] == z)
        def _():
            w_cast(i, across, bx_s, bx_r).wait_recv()
            w_cast(i, twin, bc_s, bc_r).start()

        @pl.when((across[1] != z) & jnp.logical_not(root))
        def _():
            w_cast(i, twin, bc_s, bc_r).wait_recv()

    def w_step(t):
        for h in range(deep):
            if 0 <= t - h < LUMPS:
                w_chain(t - h, h)

    loads["ch"].wait()
    loads["he"].wait()
    v_start()
    loads["st"].wait()
    loads["cot"].wait()
    w_compute()
    load_wi.start()
    loads["sc"].wait()
    loads["wo"].wait()
    exchange(0, 0)
    w_step(0)
    loads["nt"].wait()
    loads["pg"].wait()
    weigh(0)
    y_start(0)
    v_sum()
    w_step(1)
    exchange(0, 1)
    w_step(2)
    load_wi.wait()
    exchange(1, 0)
    w_step(3)
    v_total()
    weigh(1)
    y_start(1)
    w_step(4)
    exchange(1, 1)
    w_step(5)
    y_add(0)
    hop(0, 1)
    weigh(2)
    y_start(2)
    w_step(6)
    hop(0, 2)
    weigh(3)
    y_start(3)
    weigh(4)
    y_start(4)
    w_step(7)
    hop(0, 3)
    y_add(1)
    hop(1, 1)
    w_step(8)
    finish(0)
    hop(1, 2)
    hop(1, 3)
    y_add(2)
    hop(2, 1)
    finish(1)
    hop(2, 2)
    x_finish(0, out_o)
    y_add(3)
    hop(3, 1)
    y_add(4)
    hop(4, 1)
    hop(2, 3)
    hop(3, 2)
    hop(4, 2)
    finish(2)
    hop(3, 3)
    hop(4, 3)
    finish(3)
    finish(4)
    x_finish(1, ng_o)
    v_spread()
    for i in range(LUMPS):
        w_spread(i)
    for n in (1, 2):
        v_seq(n, twin[1], twin).wait_recv()
    keep = pltpu.make_async_copy(vall, sm_o, out.at[0])
    keep.start()
    for k in range(PARTS):
        spread(k)
    for k in range(PARTS):
        for n in range(2):
            spot = g_spot(twin[1], k)
            send(spot, spot, gc_s.at[n, k], gc_r.at[n, k], twin).wait_recv()
        pltpu.make_async_copy(g_spot(s, k), g_spot(s, k), loc.at[9 + k]).wait()
    keep.wait()
    v_seq(0, s, across).wait_send()
    v_seq(1, s, twin).wait_send()
    v_seq(2, s, twin).wait_send()
    for n, dst in both:
        for q in range(2):
            x_send(n, q).wait_send()
            pltpu.make_async_copy(xr.at[n, q], dst.at[q], out.at[2 + 2 * n + q]).wait()
    for q in range(2):
        twin_send(1, 1, q).wait_send()
    for k in range(PARTS):
        for e in range(deep):
            y_send(k, e).wait_send()

            @pl.when(z < e)
            def _():
                z_send(k, e, e, su, up).wait_send()

            @pl.when(z > e)
            def _():
                z_send(k, e, e, sd, down).wait_send()

        spot = g_spot(s, k)
        send(spot, spot, gx_s.at[k], gx_r.at[k], across).wait_send()
        for n in range(2):
            send(spot, spot, gc_s.at[n, k], gc_r.at[n, k], twin).wait_send()
    for i in range(LUMPS):
        wy_send(i).wait_send()

        @pl.when(z < s)
        def _():
            from_below(i).wait_send()

        @pl.when(z > s)
        def _():
            from_above(i).wait_send()

        @pl.when(root)
        def _():
            w_keep(i).wait()
            w_root(i, across, bx_s, bx_r).wait_send()

        @pl.when(root | (across[1] == z))
        def _():
            w_cast(i, twin, bc_s, bc_r).wait_send()


def scatter(normed_t, pg, scaled_t, scaled, cot, wo, wi, chacc, hacc, length, shards, groups):
    model, count = normed_t.shape
    total = pg.shape[1]
    inner = scaled_t.shape[0]
    seqs = count // length
    part = length // groups
    deep = shards // 2
    rows = model // shards
    any_ = pl.BlockSpec(memory_space=pl.ANY)
    dma = pltpu.SemaphoreType.DMA
    v = pltpu.VMEM
    small = (8, chacc.shape[2])
    return pl.pallas_call(
        functools.partial(scatter_kernel, (deep, rows, part, length)),
        in_specs=[any_] * 9,
        out_specs=[any_] * 5,
        out_shape=[
            jax.ShapeDtypeStruct((groups, rows, total), BF16),
            jax.ShapeDtypeStruct((inner // 2, model), BF16),
            jax.ShapeDtypeStruct((seqs, part, model), BF16),
            jax.ShapeDtypeStruct((seqs, part, model), BF16),
            jax.ShapeDtypeStruct((groups, *small), F32),
        ],
        scratch_shapes=[
            v((model, count), BF16),
            v((count, total), BF16),
            v((inner, count), BF16),
            v((count, inner), BF16),
            v((inner, model), BF16),
            v((count, total), BF16),
            v((model, total), BF16),
            v((deep * rows, total), BF16),
            v(((deep + 1) * rows, total), BF16),
            v((2, 2, 2, part, model), BF16),
            v((2, 2, part, model), BF16),
            v((2, part, model), BF16),
            v((inner, model), BF16),
            v((inner // 2, model), BF16),
            v((2, inner // 2, model), BF16),
            v(chacc.shape, F32),
            v(hacc.shape, F32),
            v(small, F32),
            v((deep + 1, *small), F32),
            v((groups, *small), F32),
            dma((PARTS, deep)), dma((PARTS, deep)), dma((PARTS, deep)), dma((PARTS, deep)),
            dma((PARTS, deep + 1)),
            dma((PARTS,)), dma((PARTS,)), dma((2, PARTS)), dma((2, PARTS)),
            dma((2,)), dma((2, 2, 2)), dma((2, 2)), dma((2, 2)),
            dma((LUMPS,)), dma((LUMPS,)), dma((LUMPS,)), dma((LUMPS,)), dma((2, LUMPS)),
            dma((LUMPS,)), dma((LUMPS,)), dma((LUMPS,)), dma((LUMPS,)),
            dma((deep + 4,)), dma((deep + 4,)),
            dma((9 + PARTS + LUMPS,)), dma((6,)),
        ],
        compiler_params=pltpu.CompilerParams(
            collective_id=2, has_side_effects=True, vmem_limit_bytes=60 * 2**20
        ),
        name="weigh_scatter",
    )(normed_t, pg, scaled_t, scaled, cot, wo, wi, chacc, hacc)


def local(
    tokens,
    segment_ids,
    w_in,
    w_out,
    conv_weight,
    conv_bias,
    norm_gain,
    gated_gain,
    dt_bias,
    a_log,
    skip_weight,
    cotangent,
):
    groups = lax.axis_size("seq")
    shards = lax.axis_size("dp")
    place = lax.axis_index("seq")
    owner = lax.axis_index("dp")
    seqs, part, model = tokens.shape
    length = part * groups
    rows_in = w_in.shape[0]
    rows_out = w_out.shape[0]
    wide = rows_out * shards
    heads = dt_bias.shape[0]
    size = wide // heads
    mine = heads // groups
    inner = mine * size
    span = 2 * inner
    taps = conv_weight.shape[1]
    state2 = w_in.shape[1] - 2 * wide - heads
    channels = wide + state2
    share = channels // shards
    ratio = shards // groups
    small_slice = groups == 4 and shards == 8

    def own(a):
        return lax.dynamic_slice_in_dim(a, place * inner, inner, 0)

    def own_heads(a):
        return lax.dynamic_slice_in_dim(a, place * mine, mine, 0)

    step_cols = jnp.pad(
        lax.dynamic_slice_in_dim(w_in, 2 * wide + state2 + place * mine, mine, 1),
        ((0, 0), (0, 128 - mine)),
    )
    flat = [norm_gain, conv_bias, gated_gain, conv_weight.reshape(-1)]
    small = jnp.concatenate(flat)
    tall = -(-small.shape[0] // 4096) * 4096
    small = jnp.pad(small, (0, tall - small.shape[0])).reshape(-1, 256)
    if small_slice:
        turned, cot, pj, sg, w_full, wo, small_all = gather(
            w_in, step_cols, w_out, small, tokens, cotangent, inner, shards, groups
        )
    else:
        small_all = lax.all_gather(small, "dp", axis=0, tiled=False)
    small_all = small_all.reshape(shards, -1).astype(F32)
    cut = [0]
    for a in flat:
        cut.append(cut[-1] + a.shape[0])
    norm_all, conv_b, gain_all, conv_w = (
        small_all[:, cut[i] : cut[i + 1]].reshape(-1) for i in range(4)
    )
    conv_w = conv_w.reshape(channels, taps)
    if not small_slice:
        floats = tokens.astype(F32)
        inverse = lax.rsqrt(jnp.mean(floats * floats, axis=-1, keepdims=True) + EPSILON)
        unit = floats * inverse
        w_mine = jnp.concatenate(
            [
                lax.dynamic_slice_in_dim(w_in, place * span, span, 1),
                w_in[:, 2 * wide : 2 * wide + state2],
                step_cols,
            ],
            axis=1,
        )
        normed = lax.all_gather((unit * norm_all).astype(BF16), "seq", axis=1, tiled=True)
        cot = lax.all_gather(cotangent, "seq", axis=1, tiled=True)
        w_full = lax.all_gather(w_mine, "dp", axis=0, tiled=True)
        held = jnp.where(
            (owner // ratio == place) & (jnp.arange(ratio)[:, None, None] == owner % ratio),
            w_out[None],
            jnp.zeros((), BF16),
        ).reshape(inner, model)
        wo = lax.psum(held, "dp")
        sg = jnp.einsum("std,cd->stc", cot, wo, preferred_element_type=F32).astype(BF16)
        pj = jnp.einsum("std,de->ste", normed, w_full, preferred_element_type=F32).astype(BF16)

    def pad(v):
        return jnp.pad(v, (0, 128 - mine))

    rate = -jnp.exp(own_heads(a_log))
    hp = jnp.stack([pad(own_heads(dt_bias)), pad(rate * LOG2E), pad(rate)] + [jnp.zeros(128)] * 5)
    blank = jnp.zeros((state2,), F32)
    ch = jnp.concatenate(
        [
            jnp.concatenate([own(conv_w), conv_w[wide:]]).T,
            jnp.concatenate([own(conv_b), conv_b[wide:]])[None],
            jnp.concatenate([jnp.repeat(own_heads(skip_weight), size), blank])[None],
            jnp.concatenate([own(gain_all), blank])[None],
            jnp.zeros((1, inner + state2), F32),
        ]
    )
    marks = marks_of(segment_ids)
    pre, ys, st, red = mix_forward(pj, marks, sg, hp, ch)
    if small_slice:
        rk = norms(red, wide, groups)
    else:
        totals = lax.psum(red[:, :2], "seq")
        rho = lax.rsqrt(totals[:, 0] / wide + EPSILON)
        rk = jnp.stack([rho, rho**3 * totals[:, 1] / wide] + [jnp.zeros_like(rho)] * 6, axis=1)
    pg, chacc, hacc, scaled_t, scaled = mix_backward(
        pj, marks, rk, sg, pre, ys, st, hp, ch, selectors(inner // 128)
    )
    flat_pg = pg.reshape(seqs * length, -1)
    flat_cot = cot.reshape(seqs * length, -1)
    if small_slice:
        win_grad, wo_grad, out_sum, ngrad, sums = scatter(
            turned, flat_pg, scaled_t, scaled.reshape(seqs * length, -1), flat_cot, wo, w_full,
            chacc, hacc, length, shards, groups,
        )
    else:
        product = jnp.einsum("stc,cd->std", scaled, wo, preferred_element_type=F32).astype(BF16)
        out_sum = lax.psum_scatter(product, "seq", scatter_dimension=1, tiled=True)
        product = jnp.einsum("ste,de->std", pg, w_full, preferred_element_type=F32).astype(BF16)
        ngrad = lax.psum_scatter(product, "seq", scatter_dimension=1, tiled=True)
        win_grad = jnp.einsum("std,ste->de", normed, pg, preferred_element_type=F32)
        win_grad = lax.psum_scatter(win_grad.astype(BF16), "dp", scatter_dimension=0, tiled=True)
        win_grad = lax.all_gather(win_grad, "seq", axis=0, tiled=False)
        wo_grad = jnp.dot(scaled_t, flat_cot, preferred_element_type=F32)
        wo_grad = lax.psum(wo_grad.astype(BF16), "dp").reshape(ratio, rows_out, model)
        wo_grad = lax.dynamic_index_in_dim(wo_grad, owner % ratio, 0, False)
        wo_grad = lax.psum(
            jnp.where(owner // ratio == place, wo_grad, jnp.zeros((), BF16)), "seq"
        )
        sums = jnp.concatenate(
            [
                jnp.sum(chacc, axis=1),
                jnp.pad(jnp.sum(hacc, axis=1), ((0, 0), (0, inner + state2 - 128))),
            ]
        )
        sums = lax.all_gather(lax.psum(sums, "dp"), "seq", axis=0, tiled=False)
    flat = (seqs * part, model)
    result, tokens_grad, w_in_grad, wo_grad, norm_sum, gain_sum, chan, per_head = final(
        win_grad, w_in, wo_grad, w_out, out_sum.reshape(flat), ngrad.reshape(flat),
        tokens.reshape(flat), cotangent.reshape(flat), norm_all[None], sums, span, mine, share,
    )
    return (
        result.reshape(tokens.shape),
        tokens_grad.reshape(tokens.shape),
        w_in_grad,
        wo_grad,
        chan[:share, :taps],
        chan[:share, taps],
        norm_sum[:, 0] / norm_gain.astype(F32),
        gain_sum[:, 0] / gated_gain.astype(F32),
        per_head[taps + 1, :heads],
        -jnp.exp(a_log) * per_head[taps + 2, :heads],
        per_head[taps + 3, :heads],
    )


def solution(mesh):
    return jax.shard_map(
        local,
        mesh=mesh,
        in_specs=(
            P("dp", "seq", None),
            P("dp", None),
            P("dp", None),
            P("dp", None),
            P("dp", None),
            P("dp"),
            P("dp"),
            P("dp"),
            P(),
            P(),
            P(),
            P("dp", "seq", None),
        ),
        out_specs=(
            P("dp", "seq", None),
            P("dp", "seq", None),
            P("dp", None),
            P("dp", None),
            P("dp", None),
            P("dp"),
            P("dp"),
            P("dp"),
            P(),
            P(),
            P(),
        ),
        check_vma=False,
    )
```

profile of v0, /device:TPU:3, one launch (start us, length us, event | category | flops | bytes accessed | tf_op | source)
XLA Modules:
  0.0 342.5 jit_solution(16432384260728738777)
XLA Ops:
  0.6 0.7 dynamic_slice.22
  1.4 0.7 dynamic_slice.26
  2.1 0.7 broadcast_multiply_fusion
  2.9 0.6 stack.19.hp
  3.7 0.9 constant_dynamic-slice_fusion.1
  4.5 0.6 pad.20.dt_in
  5.2 1.4 marks.1
  6.6 0.9 copy.24
  7.5 0.2 reshape.67
  7.7 2.1 concatenate.18
  9.8 0.6 reshape.68.small_in
  10.4 0.8 fusion.sel
  11.2 107.8 %gather_project.1 = (bf16[1536,2048]{1,0:T(8,128)(2,1)}, bf16[2,1024,1536]{2,1,0:T(8,128)(2,1)}, bf16[2,1024,1920]{2,1,0:T(8,128)(2,1)}, bf16[2,1024,768]{2,1,0:...) custom-call(bf16[192,6448]{1,0:T(8,128)(2,1)} %w_in.3, ...), custom_call_target="tpu_custom_call" | custom-call | tf_op jit(solution)/shard_map/gather_project/pallas_call | solution.py:889
  119.1 0.9 convert_bitcast_fusion
  120.0 0.7 broadcast_in_dim_reshape.3.gains
  121.2 1.7 reshape_reshape.3
  123.0 0.1 copy.28
  123.3 0.6 concatenate.23.ch
  123.9 25.4 %mix_forward.1 = (f32[2,1024,1024]{2,1,0:T(8,128)}, f32[2,1024,768]{2,1,0:T(8,128)}, bf16[2,8,128,768]{3,2,1,0:T(8,128)(2,1)}, f32[2,8,1024]{2,1,0:T(8,128)}) custom-call(bf16[2,1024,1920]{2,1,0:T(8,128)(2,1)} %get-tuple-element.41.pj, f32[2,8,1024]{2,1,0:T(8,128)} %marks.1, bf16[2,1024,768]{2,1,0:T(8,128)(2,1)} %get-tuple-element.42.sg, ...), custom_call_target="tpu_custom_call" | custom-call | tf_op jit(solution)/shard_map/mix_forward/pallas_call | solution.py:132
  149.3 6.8 %norms.1.rk = f32[2,8,1024]{2,1,0:T(8,128)} custom-call(f32[2,8,1024]{2,1,0:T(8,128)} %get-tuple-element.44.red), custom_call_target="tpu_custom_call" | custom-call | tf_op jit(solution)/shard_map/norms/pallas_call | solution.py:430
  156.1 46.5 %mix_backward.1 = (bf16[2,1024,1920]{2,1,0:T(8,128)(2,1)}, f32[5,8,1024]{2,1,0:T(8,128)}, f32[3,8,128]{2,1,0:T(8,128)}, bf16[768,2048]{1,0:T(8,128)(2,1)}, bf16[2,1024,768]{2,1,0:T(8,128)(2,1)}) custom-call(bf16[2,1024,1920]{2,1,0:T(8,128)(2,1)} %get-tuple-element.41.pj, f32[2,8,1024]{2,1,0:T(8,128)} %marks.1, f32[2,8,1024]{2,1,0:T(8,128)} %norms.1.rk, ...), custom_call_target="tpu_custom_call" | custom-call | tf_op jit(solution)/shard_map/mix_backward/pallas_call | solution.py:326
  202.6 120.4 %weigh_scatter.1 = (bf16[4,192,1920]{2,1,0:T(8,128)(2,1)}, bf16[384,1536]{1,0:T(8,128)(2,1)}, bf16[2,256,1536]{2,1,0:T(8,128)(2,1)}, bf16[2,256,1536]{2,1,0:T(8,128)(2,1)}, f32[4,8,1024]{2,1,0:T(8,128)}) custom-call(bf16[1536,2048]{1,0:T(8,128)(2,1)} %get-tuple-element.40.nt_in, bf16[2048,1920]{1,0:T(8,128)(2,1)} %bitcast.29, ...), custom_call_target="tpu_custom_call" | custom-call | tf_op jit(solution)/shard_map/weigh_scatter/pallas_call | solution.py:1386
  323.1 10.0 %final.1 = (bf16[512,1536]{1,0:T(8,128)(2,1)}, f32[512,1536]{1,0:T(8,128)}, f32[192,6448]{1,0:T(8,128)}, f32[384,1536]{1,0:T(8,128)}, f32[192,128]{1,0:T(8,128)}...) custom-call(bf16[4,192,1920]{2,1,0:T(8,128)(2,1)} %get-tuple-element.56.gw, bf16[192,6448]{1,0:T(8,128)(2,1)} %w_in.3, ...), custom_call_target="tpu_custom_call" | custom-call | tf_op jit(solution)/shard_map/final/pallas_call | solution.py:514
  333.1 1.2 bitcast_multiply_fusion
  334.3 1.3 slice_bitcast_fusion
  335.6 1.0 slice_reduce_fusion.2
  336.6 0.6 convert_divide_fusion.1
  337.2 1.1 slice_reduce_fusion.1
  338.2 0.6 convert_divide_fusion
  338.8 1.7 slice_reduce_fusion
  340.6 0.9 slice.45
  341.5 0.7 copy.27
  (34 shorter events, 0.9 us)
Async XLA Ops:
  323.0 10.1 %copy-start.2 = (f32[48]{0:T(128)S(1)}, f32[48]{0:T(128)}, u32[]{:S(2)}) copy-start(f32[48]{0:T(128)} %param.21) | copy-start | bytes 580
  323.0 13.5 %copy-start.1 = (bf16[192]{0:T(256)(128)(2,1)S(1)}, bf16[192]{0:T(256)(128)(2,1)}, u32[]{:S(2)}) copy-start(bf16[192]{0:T(256)(128)(2,1)} %param.18) | copy-start | bytes 1156
  323.1 15.2 %copy-start = (bf16[384]{0:T(512)(128)(2,1)S(1)}, bf16[384]{0:T(512)(128)(2,1)}, u32[]{:S(2)}) copy-start(bf16[384]{0:T(512)(128)(2,1)} %param.19) | copy-start | bytes 2308
where the time goes:
time: 347 us; the launch traced here: 343 us
  Pallas kernels  318 us (92%)
  local copies, waits for them, and re-layouts  18.2 us (5%)
  other arithmetic  4.81 us (1%)
    pallas_call x1, Pallas kernels, scatter(): pl.pallas_call(functools.partial(scatter_kernel, (deep, rows, part, lengt...  120 us
    pallas_call x1, Pallas kernels, gather(): pl.pallas_call(functools.partial(gather_kernel, (deep, pieces, rows, inne...  108 us
    pallas_call x1, Pallas kernels, mix_backward(): pl.pallas_call(functools.partial(bwd_kernel, pairs), grid=(seqs, chunks),...  46.5 us
    pallas_call x1, Pallas kernels, mix_forward(): pl.pallas_call(functools.partial(fwd_kernel, pairs), grid=(seqs, chunks),...  25.4 us
    pallas_call x1, Pallas kernels, final(): pl.pallas_call(functools.partial(final_kernel, groups, span, mine, share)...  10 us

commit v1 on v0

--- a/solution.py
+++ b/solution.py
@@ -363,7 +363,23 @@
     )(pj, marks, rk, sg, pre, ys, st, hp, ch, sel)
 
 
-def marks_kernel(seg, marks):
+def prep_kernel(mine, at, seg, heads, cols, marks, hp, sel, steps):
+    lane8 = lax.broadcasted_iota(jnp.int32, (8, 128), 1)
+    shift = 128 - lax.axis_index("seq") * mine
+    own = jnp.where(lane8 < mine, pltpu.roll(heads[...], shift, 1), 0.0)
+    rate = jnp.where(lane8 < mine, -jnp.exp(own), 0.0)[1:2, :]
+    hp[...] = jnp.concatenate([own[0:1, :], rate * LOG2E, rate, jnp.zeros((5, 128), F32)], axis=0)
+    last = cols[:, at:].astype(F32)
+    last = jnp.concatenate(
+        [last, jnp.zeros((last.shape[0], 128 - last.shape[1]), F32)], axis=1
+    )
+    lane = lax.broadcasted_iota(jnp.int32, last.shape, 1)
+    moved = pltpu.roll(last, shift, 1)
+    steps[...] = jnp.where(lane < mine, moved, 0.0).astype(BF16)
+    lane = lax.broadcasted_iota(jnp.int32, (128, 128), 0)
+    out = lax.broadcasted_iota(jnp.int32, (128, 128), 1)
+    for p in range(sel.shape[0]):
+        sel[p] = jnp.where(out == 2 * p + lane // 64, 1.0, 0.0).astype(BF16)
     seqs, length = seg.shape
     ids = seg[...].astype(F32)
     lane = lax.broadcasted_iota(jnp.int32, (seqs, length), 1)
@@ -383,19 +399,29 @@
         marks[n] = jnp.concatenate([r[n : n + 1, :] for r in all_rows], axis=0)
 
 
-def marks_of(seg):
+def prepare(seg, heads, w_in, mine, at):
+    rows = w_in.shape[0]
+    pairs = mine // 2
+    shapes = [
+        ((seg.shape[0], 8, seg.shape[1]), F32), ((8, 128), F32), ((pairs, 128, 128), BF16),
+        ((rows, 128), BF16),
+    ]
+
+    def whole(shape):
+        return pl.BlockSpec(shape, lambda i: (0,) * len(shape))
+
     return pl.pallas_call(
-        marks_kernel,
-        out_shape=jax.ShapeDtypeStruct((seg.shape[0], 8, seg.shape[1]), F32),
-        name="marks",
-    )(seg)
-
-
-def selectors(pairs):
-    lane = lax.broadcasted_iota(jnp.int32, (pairs, 128, 128), 1)
-    pair = lax.broadcasted_iota(jnp.int32, (pairs, 128, 128), 0)
-    out = lax.broadcasted_iota(jnp.int32, (pairs, 128, 128), 2)
-    return (out == 2 * pair + lane // 64).astype(BF16)
+        functools.partial(prep_kernel, mine, at),
+        grid=(1,),
+        in_specs=[
+            whole(seg.shape),
+            whole(heads.shape),
+            whole(w_in.shape),
+        ],
+        out_specs=[whole(n) for n, _ in shapes],
+        out_shape=[jax.ShapeDtypeStruct(*n) for n in shapes],
+        name="prepare",
+    )(seg, heads, w_in)
 
 
 def norm_kernel(wide, red, rk, got, ssem, rsem):
@@ -443,10 +469,12 @@
 
 
 def final_kernel(
-    groups, span, mine, share, gw, w_in, wog, w_out, osum, ngrad, tok, cot, gains, sums,
-    res, tgrad, wig, wgr, nsum, gsum, chan, head,
+    groups, span, mine, gw, w_in, wog, w_out, osum, ngrad, tok, cot, gains, sums, nrow, grow, log,
+    res, tgrad, wig, wgr, nout, gout, cout, bout, hout, nsum, gsum,
 ):
-    @pl.when(pl.program_id(0) == 0)
+    step = pl.program_id(0)
+
+    @pl.when(step == 0)
     def _():
         inner = span // 2
         shared = sums[0, :, inner:]
@@ -455,10 +483,16 @@
             shared = shared + sums[g, :, inner:]
             heads = heads + pltpu.roll(sums[g, :, :128], g * mine, 1)
         row = jnp.concatenate([*[sums[g, :, :inner] for g in range(groups)], shared], axis=1)
+        share, taps = cout.shape
         first = lax.axis_index("dp") * share
-        own = pltpu.roll(row, row.shape[1] - first, 1)[:, : chan.shape[0]]
-        chan[...] = own.T
-        head[...] = heads
+        tall = -(-share // 128) * 128
+        own = pltpu.roll(row, row.shape[1] - first, 1)[:, :tall]
+        cout[...] = own.T[:share, :taps]
+        bout[...] = own[taps : taps + 1, :share]
+        count = groups * mine
+        hout[0:1, :] = heads[taps + 1 : taps + 2, :count]
+        hout[1:2, :] = -jnp.exp(log[...]) * heads[taps + 2 : taps + 3, :count]
+        hout[2:3, :] = heads[taps + 3 : taps + 4, :count]
 
     total = jnp.zeros((w_in.shape[0], 1), F32)
     for g in range(groups):
@@ -480,12 +514,20 @@
     total = total + jnp.sum(
         steps[:, : groups * mine] * w_in[:, mid:].astype(F32), axis=1, keepdims=True
     )
-    nsum[...] = jnp.broadcast_to(total, nsum.shape)
+    tall = w_in.shape[0]
+    nsum[pl.ds(pl.multiple_of(step * tall, 16), tall), :] = jnp.broadcast_to(total, (tall, 128))
     grad = wog[...].astype(F32)
     wgr[...] = grad
-    gsum[...] = jnp.broadcast_to(
-        jnp.sum(grad * w_out[...].astype(F32), axis=1, keepdims=True), gsum.shape
+    tall = wog.shape[0]
+    gsum[pl.ds(pl.multiple_of(step * tall, 16), tall), :] = jnp.broadcast_to(
+        jnp.sum(grad * w_out[...].astype(F32), axis=1, keepdims=True), (tall, 128)
     )
+
+    @pl.when(step == pl.num_programs(0) - 1)
+    def _():
+        nout[...] = nsum[...].T[0:1, : nout.shape[1]] / nrow[...].astype(F32)
+        gout[...] = gsum[...].T[0:1, : gout.shape[1]] / grow[...].astype(F32)
+
     x = tok[...].astype(F32)
     res[...] = (x + osum[...].astype(F32)).astype(BF16)
     inverse = lax.rsqrt(jnp.mean(x * x, axis=1, keepdims=True) + EPSILON)
@@ -496,39 +538,41 @@
     )
 
 
-def final(gw, w_in, wog, w_out, osum, ngrad, tok, cot, gains, sums, span, mine, share):
-    groups, rows, total = gw.shape
-    steps = next(n for n in (4, 2, 1) if rows % (16 * n) == 0)
+def final(gw, w_in, wog, w_out, osum, ngrad, tok, cot, rows, span, mine, taps, share):
+    groups, count, total = gw.shape
+    steps = next(n for n in (4, 2, 1) if count % (16 * n) == 0)
 
     def part(a):
         return pl.BlockSpec((a.shape[0] // steps, a.shape[1]), lambda i: (i, 0))
 
+    def whole(a):
+        return pl.BlockSpec(a.shape, lambda i: (0,) * len(a.shape))
+
+    def up(n):
+        return -(-n // 128) * 128
+
     tall = [w_in, wog, w_out, osum, ngrad, tok, cot]
-    shapes = [
-        (tok.shape, BF16), (tok.shape, F32), (w_in.shape, F32), (wog.shape, F32),
-        ((rows, 128), F32), ((wog.shape[0], 128), F32),
-    ]
-    outs = [jax.ShapeDtypeStruct(*n) for n in shapes]
-    chan = jax.ShapeDtypeStruct((-(-share // 128) * 128, 8), F32)
-    head = jax.ShapeDtypeStruct((8, 128), F32)
+    big = [(tok.shape, BF16), (tok.shape, F32), (w_in.shape, F32), (wog.shape, F32)]
+    little = [(1, count), (1, wog.shape[0]), (share, taps), (1, share), (3, groups * mine)]
+    outs = [jax.ShapeDtypeStruct(*n) for n in big]
+    extra = [jax.ShapeDtypeStruct(n, F32) for n in little]
     return pl.pallas_call(
-        functools.partial(final_kernel, groups, span, mine, share),
+        functools.partial(final_kernel, groups, span, mine),
         grid=(steps,),
         in_specs=[
-            pl.BlockSpec((groups, rows // steps, total), lambda i: (0, i, 0)),
+            pl.BlockSpec((groups, count // steps, total), lambda i: (0, i, 0)),
             *[part(a) for a in tall],
-            pl.BlockSpec(gains.shape, lambda i: (0, 0)),
-            pl.BlockSpec(sums.shape, lambda i: (0, 0, 0)),
+            *[whole(a) for a in rows],
         ],
-        out_specs=[
-            *[part(o) for o in outs],
-            pl.BlockSpec(chan.shape, lambda i: (0, 0)),
-            pl.BlockSpec(head.shape, lambda i: (0, 0)),
+        out_specs=[*[part(o) for o in outs], *[whole(o) for o in extra]],
+        out_shape=[*outs, *extra],
+        scratch_shapes=[
+            pltpu.VMEM((up(count), 128), F32),
+            pltpu.VMEM((up(wog.shape[0]), 128), F32),
         ],
-        out_shape=[*outs, chan, head],
         compiler_params=pltpu.CompilerParams(vmem_limit_bytes=60 * 2**20),
         name="final",
-    )(gw, *tall, gains, sums)
+    )(gw, *tall, *rows)
 
 
 def gather_kernel(
@@ -943,7 +987,7 @@
     lax.fori_loop(0, count // some, step, 0)
 
 
-CUTS = ((0, 512), (512, 512), (1536, 384), (1024, 256), (1280, 256))
+CUTS = ((0, 512), (512, 512), (1536, 384), (1024, 256), (1280, 128), (1408, 128))
 PARTS = len(CUTS)
 
 
@@ -1282,8 +1326,9 @@
     hop(0, 2)
     weigh(3)
     y_start(3)
-    weigh(4)
-    y_start(4)
+    for k in range(4, PARTS):
+        weigh(k)
+        y_start(k)
     w_step(7)
     hop(0, 3)
     y_add(1)
@@ -1299,16 +1344,21 @@
     x_finish(0, out_o)
     y_add(3)
     hop(3, 1)
+    hop(2, 3)
     y_add(4)
     hop(4, 1)
-    hop(2, 3)
     hop(3, 2)
+    finish(2)
+    y_add(5)
+    hop(5, 1)
+    hop(3, 3)
     hop(4, 2)
-    finish(2)
-    hop(3, 3)
+    hop(5, 2)
+    finish(3)
     hop(4, 3)
-    finish(3)
+    hop(5, 3)
     finish(4)
+    finish(5)
     x_finish(1, ng_o)
     v_spread()
     for i in range(LUMPS):
@@ -1472,10 +1522,8 @@
     def own_heads(a):
         return lax.dynamic_slice_in_dim(a, place * mine, mine, 0)
 
-    step_cols = jnp.pad(
-        lax.dynamic_slice_in_dim(w_in, 2 * wide + state2 + place * mine, mine, 1),
-        ((0, 0), (0, 128 - mine)),
-    )
+    head_rows = jnp.pad(jnp.stack([dt_bias, a_log]), ((0, 6), (0, 128 - heads)))
+    marks, hp, sel, step_cols = prepare(segment_ids, head_rows, w_in, mine, 2 * wide + state2)
     flat = [norm_gain, conv_bias, gated_gain, conv_weight.reshape(-1)]
     small = jnp.concatenate(flat)
     tall = -(-small.shape[0] // 4096) * 4096
@@ -1518,11 +1566,6 @@
         sg = jnp.einsum("std,cd->stc", cot, wo, preferred_element_type=F32).astype(BF16)
         pj = jnp.einsum("std,de->ste", normed, w_full, preferred_element_type=F32).astype(BF16)
 
-    def pad(v):
-        return jnp.pad(v, (0, 128 - mine))
-
-    rate = -jnp.exp(own_heads(a_log))
-    hp = jnp.stack([pad(own_heads(dt_bias)), pad(rate * LOG2E), pad(rate)] + [jnp.zeros(128)] * 5)
     blank = jnp.zeros((state2,), F32)
     ch = jnp.concatenate(
         [
@@ -1533,7 +1576,6 @@
             jnp.zeros((1, inner + state2), F32),
         ]
     )
-    marks = marks_of(segment_ids)
     pre, ys, st, red = mix_forward(pj, marks, sg, hp, ch)
     if small_slice:
         rk = norms(red, wide, groups)
@@ -1542,7 +1584,7 @@
         rho = lax.rsqrt(totals[:, 0] / wide + EPSILON)
         rk = jnp.stack([rho, rho**3 * totals[:, 1] / wide] + [jnp.zeros_like(rho)] * 6, axis=1)
     pg, chacc, hacc, scaled_t, scaled = mix_backward(
-        pj, marks, rk, sg, pre, ys, st, hp, ch, selectors(inner // 128)
+        pj, marks, rk, sg, pre, ys, st, hp, ch, sel
     )
     flat_pg = pg.reshape(seqs * length, -1)
     flat_cot = cot.reshape(seqs * length, -1)
@@ -1573,22 +1615,25 @@
         )
         sums = lax.all_gather(lax.psum(sums, "dp"), "seq", axis=0, tiled=False)
     flat = (seqs * part, model)
-    result, tokens_grad, w_in_grad, wo_grad, norm_sum, gain_sum, chan, per_head = final(
-        win_grad, w_in, wo_grad, w_out, out_sum.reshape(flat), ngrad.reshape(flat),
-        tokens.reshape(flat), cotangent.reshape(flat), norm_all[None], sums, span, mine, share,
+    rows = [norm_all[None], sums, norm_gain[None], gated_gain[None], a_log[None]]
+    (result, tokens_grad, w_in_grad, wo_grad, norm_grad, gain_grad, conv_grad, bias_grad, per_head) = (
+        final(
+            win_grad, w_in, wo_grad, w_out, out_sum.reshape(flat), ngrad.reshape(flat),
+            tokens.reshape(flat), cotangent.reshape(flat), rows, span, mine, taps, share,
+        )
     )
     return (
         result.reshape(tokens.shape),
         tokens_grad.reshape(tokens.shape),
         w_in_grad,
         wo_grad,
-        chan[:share, :taps],
-        chan[:share, taps],
-        norm_sum[:, 0] / norm_gain.astype(F32),
-        gain_sum[:, 0] / gated_gain.astype(F32),
-        per_head[taps + 1, :heads],
-        -jnp.exp(a_log) * per_head[taps + 2, :heads],
-        per_head[taps + 3, :heads],
+        conv_grad,
+        bias_grad[0],
+        norm_grad[0],
+        gain_grad[0],
+        per_head[0],
+        per_head[1],
+        per_head[2],
     )
 
 

time: 347 us -> 342 us (0.986)
  local copies, waits for them, and re-layouts: 18.2 us -> 14 us
    slice x4 -> x0, local copies, waits for them, and re-layouts: 4.75 us -> none  [the longest x1 1.74 us: local(): chan[:share, taps]]
where the time goes in v1:
time: 342 us; the launch traced here: 338 us
  Pallas kernels  320 us (94%)
  local copies, waits for them, and re-layouts  14 us (4%)
    pallas_call x1, Pallas kernels, scatter(): pl.pallas_call(functools.partial(scatter_kernel, (deep, rows, part, lengt...  121 us
    pallas_call x1, Pallas kernels, gather(): pl.pallas_call(functools.partial(gather_kernel, (deep, pieces, rows, inne...  108 us
    pallas_call x1, Pallas kernels, mix_backward(): pl.pallas_call(functools.partial(bwd_kernel, pairs), grid=(seqs, chunks),...  46.5 us
    pallas_call x1, Pallas kernels, mix_forward(): pl.pallas_call(functools.partial(fwd_kernel, pairs), grid=(seqs, chunks),...  25.4 us
    pallas_call x1, Pallas kernels, final(): pl.pallas_call(functools.partial(final_kernel, groups, span, mine), grid=...  10.2 us

profile of v1, /device:TPU:3, one launch (start us, length us, event | category | flops | bytes accessed | tf_op | source)
XLA Modules:
  0.0 338.4 jit_solution(4529153554513266049)
XLA Ops:
  0.6 0.7 dynamic_slice.14
  1.4 1.2 broadcast_in_dim.28.nrow
  2.6 1.3 broadcast_in_dim.29.grow
  3.9 1.3 select_maximum_fusion.heads
  5.2 0.1 reshape.70
  5.3 0.9 copy.24
  6.2 0.2 reshape.67
  6.3 2.1 concatenate.18
  8.5 0.6 reshape.68.small_in
  9.1 2.6 prepare.1
  11.7 107.8 %gather_project.1 = (bf16[1536,2048]{1,0:T(8,128)(2,1)}, bf16[2,1024,1536]{2,1,0:T(8,128)(2,1)}, bf16[2,1024,1920]{2,1,0:T(8,128)(2,1)}, bf16[2,1024,768]{2,1,0:...) custom-call(bf16[192,6448]{1,0:T(8,128)(2,1)} %w_in.3, ...), custom_call_target="tpu_custom_call" | custom-call | tf_op jit(solution)/shard_map/gather_project/pallas_call | solution.py:933
  119.5 0.9 convert_bitcast_fusion
  120.4 0.1 copy.30
  120.5 0.7 broadcast_in_dim_reshape.3.gains
  121.1 0.1 slice.40
  121.2 0.1 dynamic_slice.15
  121.3 0.1 slice.38
  121.4 0.1 slice.36
  121.4 0.1 reshape.69
  121.5 0.1 dynamic_slice.13
  121.6 1.7 reshape_reshape.3
  123.4 0.1 copy.28
  123.6 0.1 copy.29
  123.7 0.6 concatenate.23.ch
  124.3 25.4 %mix_forward.1 = (f32[2,1024,1024]{2,1,0:T(8,128)}, f32[2,1024,768]{2,1,0:T(8,128)}, bf16[2,8,128,768]{3,2,1,0:T(8,128)(2,1)}, f32[2,8,1024]{2,1,0:T(8,128)}) custom-call(bf16[2,1024,1920]{2,1,0:T(8,128)(2,1)} %get-tuple-element.47.pj, f32[2,8,1024]{2,1,0:T(8,128)} %get-tuple-element.48.marks, bf16[2,1024,768]{2,1,0:T(8,128)(2,1)} %get-tuple-element.49.sg, ...), custom_call_target="tpu_custom_call" | custom-call | tf_op jit(solution)/shard_map/mix_forward/pallas_call | solution.py:132
  149.8 6.8 %norms.1.rk = f32[2,8,1024]{2,1,0:T(8,128)} custom-call(f32[2,8,1024]{2,1,0:T(8,128)} %get-tuple-element.52.red), custom_call_target="tpu_custom_call" | custom-call | tf_op jit(solution)/shard_map/norms/pallas_call | solution.py:456
  156.6 46.5 %mix_backward.1 = (bf16[2,1024,1920]{2,1,0:T(8,128)(2,1)}, f32[5,8,1024]{2,1,0:T(8,128)}, f32[3,8,128]{2,1,0:T(8,128)}, bf16[768,2048]{1,0:T(8,128)(2,1)}, bf16[2,1024,768]{2,1,0:T(8,128)(2,1)}) custom-call(bf16[2,1024,1920]{2,1,0:T(8,128)(2,1)} %get-tuple-element.47.pj, f32[2,8,1024]{2,1,0:T(8,128)} %get-tuple-element.48.marks, f32[2,8,1024]{2,1,0:T(8,128)} %norms.1.rk, ...), custom_call_target="tpu_custom_call" | custom-call | tf_op jit(solution)/shard_map/mix_backward/pallas_call | solution.py:326
  203.1 120.6 %weigh_scatter.1 = (bf16[4,192,1920]{2,1,0:T(8,128)(2,1)}, bf16[384,1536]{1,0:T(8,128)(2,1)}, bf16[2,256,1536]{2,1,0:T(8,128)(2,1)}, bf16[2,256,1536]{2,1,0:T(8,128)(2,1)}, f32[4,8,1024]{2,1,0:T(8,128)}) custom-call(bf16[1536,2048]{1,0:T(8,128)(2,1)} %get-tuple-element.46.nt_in, bf16[2048,1920]{1,0:T(8,128)(2,1)} %bitcast.27, ...), custom_call_target="tpu_custom_call" | custom-call | tf_op jit(solution)/shard_map/weigh_scatter/pallas_call | solution.py:1436
  323.7 10.2 %final.1 = (bf16[512,1536]{1,0:T(8,128)(2,1)}, f32[512,1536]{1,0:T(8,128)}, f32[192,6448]{1,0:T(8,128)}, f32[384,1536]{1,0:T(8,128)}, f32[1,192]{1,0:T(1,128)}, ...) custom-call(bf16[4,192,1920]{2,1,0:T(8,128)(2,1)} %get-tuple-element.65.gw, ...), custom_call_target="tpu_custom_call" | custom-call | tf_op jit(solution)/shard_map/final/pallas_call | solution.py:559
  333.9 1.3 slice_bitcast_fusion
  335.2 1.3 reduce
  336.5 1.6 copy.27
  (12 shorter events, 0.2 us)

commit v2 on v1

--- a/solution.py
+++ b/solution.py
@@ -579,13 +579,14 @@
     dims, w_in, dt_in, wo_in, small_in, tok_in, cot_in,
     turned_o, cot_o, pj_o, sg_o, w_o, wo_o, small_o,
     tok, cot, wbig, wo, small, pjv, sgv, turned,
-    szu, szd, rz, sy, ry, wsu, wsd, wrz, wsy, wry, bx_s, bx_r, bc_s, bc_r, loc, out,
+    szu, szd, rz, sy, ry, wsu, wsd, wrz, wsy, wry, bx_s, bx_r, bc_s, bc_r, bs, br, loc, out,
 ):
     deep, pieces, rows, inner, part, length, groups = dims
     d = lax.axis_index("dp")
     s = lax.axis_index("seq")
     z = d // 2
     y = d % 2
+    core = s % 2
     top = deep - 1
     up, down, side = (d + 2, s), (d - 2, s), (d + 1 - 2 * y, s)
     across, twin = (d, s + 2 - 4 * (s // 2)), (d, s + 1 - 2 * (s % 2))
@@ -619,7 +620,28 @@
     def held(k, owner):
         if k == 0:
             return small.at[owner]
+        if k == 2:
+            return shared(owner, core)
         return wbig.at[pl.ds(pl.multiple_of(owner * rows, 16), rows), cols(k)]
+
+    def shared(owner, half):
+        at = pl.multiple_of(owner * rows + half * (rows // 2), 16)
+        return wbig.at[pl.ds(at, rows // 2), pl.ds(width, 256)]
+
+    def shared_send(owner, half):
+        ref = shared(owner, half)
+        return send(ref, ref, bs.at[owner], br.at[owner], twin)
+
+    def share_columns():
+        for e in range(2 * deep):
+            @pl.when(d != e)
+            def _():
+                shared_send(e, core).start()
+
+        for e in range(2 * deep):
+            @pl.when(d != e)
+            def _():
+                shared_send(e, 1 - core).wait_recv()
 
     def source(k):
         if k == 0:
@@ -627,7 +649,8 @@
         if k == 1:
             return dt_in.at[...]
         if k == 2:
-            return w_in.at[:, pl.ds(width * groups, 256)]
+            at = pl.multiple_of(core * (rows // 2), 16)
+            return w_in.at[pl.ds(at, rows // 2), pl.ds(width * groups, 256)]
         return w_in.at[:, pl.ds(pl.multiple_of(s * width + (k - 3) * 256, 128), 256)]
 
     def own_send(k):
@@ -689,8 +712,14 @@
     for q in range(2):
         locals_.append(own_copy(tok_in.at[q], tok.at[q, pl.ds(here, part)], loc.at[2 + q]))
         locals_.append(own_copy(cot_in.at[q], cot.at[q, pl.ds(here, part)], loc.at[4 + q]))
-    for k in (1, 2):
-        locals_.append(own_copy(source(k), held(k, d), loc.at[6 + k]))
+    locals_.append(own_copy(source(1), held(1, d), loc.at[7]))
+    locals_.append(
+        own_copy(
+            w_in.at[:, pl.ds(width * groups, 256)],
+            wbig.at[pl.ds(pl.multiple_of(d * rows, 16), rows), pl.ds(width, 256)],
+            loc.at[8],
+        )
+    )
     half = wo_in.shape[0]
     mine = z == s
 
@@ -775,6 +804,8 @@
 
     for q in range(2):
         block_sends(0, tok_in, tok, q)
+    for q in range(2):
+        block_sends(1, cot_in, cot, q)
     ahead = 3
     for k in range(ahead):
         own_send(k)
@@ -799,6 +830,8 @@
         for _ in range(n):
             if count["next"] < pieces:
                 arrive(count["next"])
+                if count["next"] == 2:
+                    share_columns()
                 if count["next"] > 1:
                     project(count["next"])
                 count["next"] += 1
@@ -834,8 +867,6 @@
             block_forward(0, tok, 0)
         if t == 6:
             block_forward(0, tok, 1)
-            for q in range(2):
-                block_sends(1, cot_in, cot, q)
         if t == 7:
             for i in (0, 1, 2, 4, 6, 7):
                 locals_[i].wait()
@@ -885,6 +916,11 @@
                 send(ref, ref, szd.at[k, e], rz.at[k, e], down).wait_send()
 
             send(ref, ref, sy.at[k, e], ry.at[k, e], side).wait_send()
+    for e in range(2 * deep):
+        @pl.when(d != e)
+        def _():
+            shared_send(e, core).wait_send()
+
     for i in range(LUMPS):
         m, ref = wo_piece(i, y)
 
@@ -948,6 +984,7 @@
             dma((pieces, deep)), dma((pieces, deep)),
             *[dma((2 * LUMPS,))] * 5,
             dma((4,)), dma((4,)), dma((2, 4)), dma((2, 4)),
+            dma((2 * deep,)), dma((2 * deep,)),
             dma((9,)), dma((pieces + 5,)),
         ],
         compiler_params=pltpu.CompilerParams(
@@ -1129,12 +1166,14 @@
             pltpu.make_async_copy(xr.at[n, q], dst.at[q], out.at[2 + 2 * n + q]).start()
 
     def weigh(k):
+        tall = 2 * rows
+
         def step(i, _):
-            at = pl.ds(pl.multiple_of(i * rows, 16), rows)
+            at = pl.ds(pl.multiple_of(i * tall, 16), tall)
             pv[at, cut(k)] = mm(nt_v[at, :], pg_v[:, cut(k)]).astype(BF16)
             return 0
 
-        lax.fori_loop(0, 2 * deep, step, 0)
+        lax.fori_loop(0, deep, step, 0)
 
     def block(e, k):
         return pv.at[pl.ds(pl.multiple_of((2 * e + y) * rows, 16), rows), cut(k)]

time: 342 us -> 340 us (level)
    pallas_call x1, Pallas kernels: 108 us -> 104 us  [gather(): pl.pallas_call(functools.partial(gather_kernel, (deep, pieces, rows, inne...]
where the time goes in v2:
time: 340 us; the launch traced here: 336 us
  Pallas kernels  318 us (94%)
  local copies, waits for them, and re-layouts  14 us (4%)
  other arithmetic  3.4 us (1%)
    pallas_call x1, Pallas kernels, scatter(): pl.pallas_call(functools.partial(scatter_kernel, (deep, rows, part, lengt...  123 us
    pallas_call x1, Pallas kernels, gather(): pl.pallas_call(functools.partial(gather_kernel, (deep, pieces, rows, inne...  104 us
    pallas_call x1, Pallas kernels, mix_backward(): pl.pallas_call(functools.partial(bwd_kernel, pairs), grid=(seqs, chunks),...  46.5 us
    pallas_call x1, Pallas kernels, mix_forward(): pl.pallas_call(functools.partial(fwd_kernel, pairs), grid=(seqs, chunks),...  25.4 us
    pallas_call x1, Pallas kernels, final(): pl.pallas_call(functools.partial(final_kernel, groups, span, mine), grid=...  10.2 us
    pallas_call x1, Pallas kernels, norms(): pl.pallas_call(functools.partial(norm_kernel, wide), in_specs=[vmem], out...  6.82 us

profile of v2, /device:TPU:3, one launch (start us, length us, event | category | flops | bytes accessed | tf_op | source)
XLA Modules:
  0.0 336.4 jit_solution(7189572131151686550)
XLA Ops:
  0.6 0.7 dynamic_slice.14
  1.4 1.2 broadcast_in_dim.28.nrow
  2.6 1.3 broadcast_in_dim.29.grow
  3.9 1.3 select_maximum_fusion.heads
  5.2 0.1 reshape.70
  5.3 0.9 copy.24
  6.2 0.2 reshape.67
  6.3 2.1 concatenate.18
  8.5 0.6 reshape.68.small_in
  9.1 2.6 prepare.1
  11.7 103.9 %gather_project.1 = (bf16[1536,2048]{1,0:T(8,128)(2,1)}, bf16[2,1024,1536]{2,1,0:T(8,128)(2,1)}, bf16[2,1024,1920]{2,1,0:T(8,128)(2,1)}, bf16[2,1024,768]{2,1,0:...) custom-call(bf16[192,6448]{1,0:T(8,128)(2,1)} %w_in.3, ...), custom_call_target="tpu_custom_call" | custom-call | tf_op jit(solution)/shard_map/gather_project/pallas_call | solution.py:969
  115.6 0.9 convert_bitcast_fusion
  116.4 0.1 copy.30
  116.5 0.7 broadcast_in_dim_reshape.3.gains
  117.2 0.1 slice.40
  117.3 0.1 dynamic_slice.15
  117.3 0.1 slice.38
  117.4 0.1 slice.36
  117.5 0.1 reshape.69
  117.6 0.1 dynamic_slice.13
  117.7 1.7 reshape_reshape.3
  119.5 0.1 copy.28
  119.6 0.1 copy.29
  119.7 0.6 concatenate.23.ch
  120.4 25.4 %mix_forward.1 = (f32[2,1024,1024]{2,1,0:T(8,128)}, f32[2,1024,768]{2,1,0:T(8,128)}, bf16[2,8,128,768]{3,2,1,0:T(8,128)(2,1)}, f32[2,8,1024]{2,1,0:T(8,128)}) custom-call(bf16[2,1024,1920]{2,1,0:T(8,128)(2,1)} %get-tuple-element.47.pj, f32[2,8,1024]{2,1,0:T(8,128)} %get-tuple-element.48.marks, bf16[2,1024,768]{2,1,0:T(8,128)(2,1)} %get-tuple-element.49.sg, ...), custom_call_target="tpu_custom_call" | custom-call | tf_op jit(solution)/shard_map/mix_forward/pallas_call | solution.py:132
  145.8 6.8 %norms.1.rk = f32[2,8,1024]{2,1,0:T(8,128)} custom-call(f32[2,8,1024]{2,1,0:T(8,128)} %get-tuple-element.52.red), custom_call_target="tpu_custom_call" | custom-call | tf_op jit(solution)/shard_map/norms/pallas_call | solution.py:456
  152.6 46.5 %mix_backward.1 = (bf16[2,1024,1920]{2,1,0:T(8,128)(2,1)}, f32[5,8,1024]{2,1,0:T(8,128)}, f32[3,8,128]{2,1,0:T(8,128)}, bf16[768,2048]{1,0:T(8,128)(2,1)}, bf16[2,1024,768]{2,1,0:T(8,128)(2,1)}) custom-call(bf16[2,1024,1920]{2,1,0:T(8,128)(2,1)} %get-tuple-element.47.pj, f32[2,8,1024]{2,1,0:T(8,128)} %get-tuple-element.48.marks, f32[2,8,1024]{2,1,0:T(8,128)} %norms.1.rk, ...), custom_call_target="tpu_custom_call" | custom-call | tf_op jit(solution)/shard_map/mix_backward/pallas_call | solution.py:326
  199.1 122.6 %weigh_scatter.1 = (bf16[4,192,1920]{2,1,0:T(8,128)(2,1)}, bf16[384,1536]{1,0:T(8,128)(2,1)}, bf16[2,256,1536]{2,1,0:T(8,128)(2,1)}, bf16[2,256,1536]{2,1,0:T(8,128)(2,1)}, f32[4,8,1024]{2,1,0:T(8,128)}) custom-call(bf16[1536,2048]{1,0:T(8,128)(2,1)} %get-tuple-element.46.nt_in, bf16[2048,1920]{1,0:T(8,128)(2,1)} %bitcast.27, ...), custom_call_target="tpu_custom_call" | custom-call | tf_op jit(solution)/shard_map/weigh_scatter/pallas_call | solution.py:1475
  321.7 10.2 %final.1 = (bf16[512,1536]{1,0:T(8,128)(2,1)}, f32[512,1536]{1,0:T(8,128)}, f32[192,6448]{1,0:T(8,128)}, f32[384,1536]{1,0:T(8,128)}, f32[1,192]{1,0:T(1,128)}, ...) custom-call(bf16[4,192,1920]{2,1,0:T(8,128)(2,1)} %get-tuple-element.65.gw, ...), custom_call_target="tpu_custom_call" | custom-call | tf_op jit(solution)/shard_map/final/pallas_call | solution.py:559
  331.9 1.3 slice_bitcast_fusion
  333.2 1.3 reduce
  334.5 1.6 copy.27
  (12 shorter events, 0.2 us)

commit v3 on v2

--- a/solution.py
+++ b/solution.py
@@ -470,7 +470,7 @@
 
 def final_kernel(
     groups, span, mine, gw, w_in, wog, w_out, osum, ngrad, tok, cot, gains, sums, nrow, grow, log,
-    res, tgrad, wig, wgr, nout, gout, cout, bout, hout, nsum, gsum,
+    res, tgrad, wig, wgr, nout, gout, cout, bout, hout0, hout1, hout2, nsum, gsum,
 ):
     step = pl.program_id(0)
 
@@ -488,11 +488,11 @@
         tall = -(-share // 128) * 128
         own = pltpu.roll(row, row.shape[1] - first, 1)[:, :tall]
         cout[...] = own.T[:share, :taps]
-        bout[...] = own[taps : taps + 1, :share]
+        bout[...] = own[taps, :share]
         count = groups * mine
-        hout[0:1, :] = heads[taps + 1 : taps + 2, :count]
-        hout[1:2, :] = -jnp.exp(log[...]) * heads[taps + 2 : taps + 3, :count]
-        hout[2:3, :] = heads[taps + 3 : taps + 4, :count]
+        hout0[...] = heads[taps + 1, :count]
+        hout1[...] = -jnp.exp(log[...]) * heads[taps + 2, :count]
+        hout2[...] = heads[taps + 3, :count]
 
     total = jnp.zeros((w_in.shape[0], 1), F32)
     for g in range(groups):
@@ -525,8 +525,8 @@
 
     @pl.when(step == pl.num_programs(0) - 1)
     def _():
-        nout[...] = nsum[...].T[0:1, : nout.shape[1]] / nrow[...].astype(F32)
-        gout[...] = gsum[...].T[0:1, : gout.shape[1]] / grow[...].astype(F32)
+        nout[...] = nsum[...].T[0, : nout.shape[0]] / nrow[...].astype(F32)
+        gout[...] = gsum[...].T[0, : gout.shape[0]] / grow[...].astype(F32)
 
     x = tok[...].astype(F32)
     res[...] = (x + osum[...].astype(F32)).astype(BF16)
@@ -553,7 +553,7 @@
 
     tall = [w_in, wog, w_out, osum, ngrad, tok, cot]
     big = [(tok.shape, BF16), (tok.shape, F32), (w_in.shape, F32), (wog.shape, F32)]
-    little = [(1, count), (1, wog.shape[0]), (share, taps), (1, share), (3, groups * mine)]
+    little = [(count,), (wog.shape[0],), (share, taps), (share,), *[(groups * mine,)] * 3]
     outs = [jax.ShapeDtypeStruct(*n) for n in big]
     extra = [jax.ShapeDtypeStruct(n, F32) for n in little]
     return pl.pallas_call(
@@ -1654,25 +1654,22 @@
         )
         sums = lax.all_gather(lax.psum(sums, "dp"), "seq", axis=0, tiled=False)
     flat = (seqs * part, model)
-    rows = [norm_all[None], sums, norm_gain[None], gated_gain[None], a_log[None]]
-    (result, tokens_grad, w_in_grad, wo_grad, norm_grad, gain_grad, conv_grad, bias_grad, per_head) = (
-        final(
-            win_grad, w_in, wo_grad, w_out, out_sum.reshape(flat), ngrad.reshape(flat),
-            tokens.reshape(flat), cotangent.reshape(flat), rows, span, mine, taps, share,
-        )
+    rows = [norm_all[None], sums, norm_gain, gated_gain, a_log]
+    outs = final(
+        win_grad, w_in, wo_grad, w_out, out_sum.reshape(flat), ngrad.reshape(flat),
+        tokens.reshape(flat), cotangent.reshape(flat), rows, span, mine, taps, share,
     )
+    result, tokens_grad, w_in_grad, wo_grad, norm_grad, gain_grad, conv_grad, bias_grad = outs[:8]
     return (
         result.reshape(tokens.shape),
         tokens_grad.reshape(tokens.shape),
         w_in_grad,
         wo_grad,
         conv_grad,
-        bias_grad[0],
-        norm_grad[0],
-        gain_grad[0],
-        per_head[0],
-        per_head[1],
-        per_head[2],
+        bias_grad,
+        norm_grad,
+        gain_grad,
+        *outs[8:],
     )
 
 

time: 340 us -> 335 us (0.985)
  local copies, waits for them, and re-layouts: 14 us -> 10.2 us
where the time goes in v3:
time: 335 us; the launch traced here: 331 us
  Pallas kernels  318 us (95%)
  local copies, waits for them, and re-layouts  10.2 us (3%)
    pallas_call x1, Pallas kernels, scatter(): pl.pallas_call(functools.partial(scatter_kernel, (deep, rows, part, lengt...  123 us
    pallas_call x1, Pallas kernels, gather(): pl.pallas_call(functools.partial(gather_kernel, (deep, pieces, rows, inne...  104 us
    pallas_call x1, Pallas kernels, mix_backward(): pl.pallas_call(functools.partial(bwd_kernel, pairs), grid=(seqs, chunks),...  46.5 us
    pallas_call x1, Pallas kernels, mix_forward(): pl.pallas_call(functools.partial(fwd_kernel, pairs), grid=(seqs, chunks),...  25.4 us
    pallas_call x1, Pallas kernels, final(): pl.pallas_call(functools.partial(final_kernel, groups, span, mine), grid=...  10.2 us
    pallas_call x1, Pallas kernels, norms(): pl.pallas_call(functools.partial(norm_kernel, wide), in_specs=[vmem], out...  6.82 us

profile of v3, /device:TPU:3, one launch (start us, length us, event | category | flops | bytes accessed | tf_op | source)
XLA Modules:
  0.0 331.3 jit_solution(15385497415656449855)
XLA Ops:
  0.6 0.7 dynamic_slice.14
  1.4 1.3 select_maximum_fusion.heads
  2.7 0.1 broadcast_in_dim.17
  2.7 0.1 reshape.70
  2.8 0.9 copy.24
  3.7 0.2 reshape.67
  3.8 2.1 concatenate.18
  6.0 0.6 reshape.68.small_in
  6.6 2.5 prepare.1
  9.1 103.9 %gather_project.1 = (bf16[1536,2048]{1,0:T(8,128)(2,1)}, bf16[2,1024,1536]{2,1,0:T(8,128)(2,1)}, bf16[2,1024,1920]{2,1,0:T(8,128)(2,1)}, bf16[2,1024,768]{2,1,0:...) custom-call(bf16[192,6448]{1,0:T(8,128)(2,1)} %w_in.3, ...), custom_call_target="tpu_custom_call" | custom-call | tf_op jit(solution)/shard_map/gather_project/pallas_call | solution.py:969
  113.1 0.9 convert_bitcast_fusion
  113.9 0.1 copy.30
  114.0 0.7 broadcast_in_dim_reshape.3.gains
  114.7 0.1 slice.28
  114.8 0.1 dynamic_slice.15
  114.8 0.1 slice.26
  114.9 0.1 slice.24
  115.0 0.1 reshape.69
  115.1 0.1 dynamic_slice.13
  115.2 1.7 reshape_reshape.3
  117.0 0.1 copy.28
  117.1 0.1 copy.29
  117.2 0.6 concatenate.23.ch
  117.9 25.4 %mix_forward.1 = (f32[2,1024,1024]{2,1,0:T(8,128)}, f32[2,1024,768]{2,1,0:T(8,128)}, bf16[2,8,128,768]{3,2,1,0:T(8,128)(2,1)}, f32[2,8,1024]{2,1,0:T(8,128)}) custom-call(bf16[2,1024,1920]{2,1,0:T(8,128)(2,1)} %get-tuple-element.49.pj, f32[2,8,1024]{2,1,0:T(8,128)} %get-tuple-element.50.marks, bf16[2,1024,768]{2,1,0:T(8,128)(2,1)} %get-tuple-element.51.sg, ...), custom_call_target="tpu_custom_call" | custom-call | tf_op jit(solution)/shard_map/mix_forward/pallas_call | solution.py:132
  143.3 6.8 %norms.1.rk = f32[2,8,1024]{2,1,0:T(8,128)} custom-call(f32[2,8,1024]{2,1,0:T(8,128)} %get-tuple-element.54.red), custom_call_target="tpu_custom_call" | custom-call | tf_op jit(solution)/shard_map/norms/pallas_call | solution.py:456
  150.1 46.5 %mix_backward.1 = (bf16[2,1024,1920]{2,1,0:T(8,128)(2,1)}, f32[5,8,1024]{2,1,0:T(8,128)}, f32[3,8,128]{2,1,0:T(8,128)}, bf16[768,2048]{1,0:T(8,128)(2,1)}, bf16[2,1024,768]{2,1,0:T(8,128)(2,1)}) custom-call(bf16[2,1024,1920]{2,1,0:T(8,128)(2,1)} %get-tuple-element.49.pj, f32[2,8,1024]{2,1,0:T(8,128)} %get-tuple-element.50.marks, f32[2,8,1024]{2,1,0:T(8,128)} %norms.1.rk, ...), custom_call_target="tpu_custom_call" | custom-call | tf_op jit(solution)/shard_map/mix_backward/pallas_call | solution.py:326
  196.6 122.6 %weigh_scatter.1 = (bf16[4,192,1920]{2,1,0:T(8,128)(2,1)}, bf16[384,1536]{1,0:T(8,128)(2,1)}, bf16[2,256,1536]{2,1,0:T(8,128)(2,1)}, bf16[2,256,1536]{2,1,0:T(8,128)(2,1)}, f32[4,8,1024]{2,1,0:T(8,128)}) custom-call(bf16[1536,2048]{1,0:T(8,128)(2,1)} %get-tuple-element.48.nt_in, bf16[2048,1920]{1,0:T(8,128)(2,1)} %bitcast.19, ...), custom_call_target="tpu_custom_call" | custom-call | tf_op jit(solution)/shard_map/weigh_scatter/pallas_call | solution.py:1475
  319.2 10.2 %final.1 = (bf16[512,1536]{1,0:T(8,128)(2,1)}, f32[512,1536]{1,0:T(8,128)}, f32[192,6448]{1,0:T(8,128)}, f32[384,1536]{1,0:T(8,128)}, f32[192]{0:T(256)}, /*inde...) custom-call(bf16[4,192,1920]{2,1,0:T(8,128)(2,1)} %get-tuple-element.67.gw, ...), custom_call_target="tpu_custom_call" | custom-call | tf_op jit(solution)/shard_map/final/pallas_call | solution.py:559
  329.4 1.6 copy.27
  (11 shorter events, 0.1 us)
